TPU v7x, 32 devices: a whole 2x2x4 slice. The times are simulated.
32 devices in a mesh: mom: 8 (over z, x), trow: 4 (over y, core).
Axes of the slice: x: 2, y: 2, z: 4, core: 2. Of those that a mesh axis runs over, the one named last changes fastest.
Arguments:
- lesser: bfloat16 [2, 256, 512, 512], P(None, 'mom', 'trow'), may hold values from -12 to 12
- greater: bfloat16 [2, 256, 512, 512], P(None, 'mom', 'trow'), may hold values from -12 to 12
- momentum_ids: int32 [256], replicated, may hold values from 0 to 255, each once
- window_start: int32 [1], replicated, may hold values from 0 to 2047
Outputs:
- collision: bfloat16 [2, 256, 512, 512], P(None, 'mom', 'trow')
Inputs may be any that keep to these rules, and one draw needn't show every extreme that they name: Position j holds lattice momentum (momentum_ids[j] // 16, momentum_ids[j] % 16); every value appears once.
All inputs are finite; a program needn't handle non-finite values.
Results may differ from a plain program's by a relative error of at most 0.009.
Values may be sent and summed in bfloat16 or wider, within the bound.
No kernel may reach another device: no remote copies, remote signals or barrier semaphores. Data moves between devices by JAX's collectives and lax.ppermute only.
A program may use at most 192 MiB of HBM per device.

v0:
```python
import jax
import jax.numpy as jnp
from jax import lax
from jax.sharding import PartitionSpec as P

LX = 16
LY = 16
DRIVE = 128


U_BASE = 4.0
TIME_STEP = 0.02


def lattice_tables(momentum_ids):
    momenta = momentum_ids.shape[0]
    wave_x = momentum_ids // LY
    wave_y = momentum_ids % LY
    sites = jnp.arange(momenta, dtype=jnp.int32)
    site_x = sites // LY
    site_y = sites % LY
    phase = (
        wave_x[:, None] * site_x[None, :] % LX * LY + wave_y[:, None] * site_y[None, :] % LY * LX
    )
    angle = 2.0 * jnp.pi / momenta * (phase % momenta).astype(jnp.float32)
    return (jnp.cos(angle), jnp.sin(angle), momenta)


def transforms(momentum_ids):
    cos_table, sin_table, momenta = lattice_tables(momentum_ids)
    forward = jnp.stack(
        [jnp.stack([cos_table, sin_table], 1), jnp.stack([-sin_table, cos_table], 1)], 0
    )
    forward = (forward / momenta).astype(jnp.bfloat16)
    backward = jnp.stack(
        [jnp.stack([cos_table.T, -sin_table.T], 1), jnp.stack([sin_table.T, cos_table.T], 1)], 0
    )
    return (forward, backward.astype(jnp.bfloat16))


def drive(window_start, row_times):
    phase = ((window_start[0] + row_times) % DRIVE).astype(jnp.float32)
    return U_BASE * (1.0 + 0.5 * jnp.sin(2.0 * jnp.pi / DRIVE * phase))


def second_born(less_part, more_part, forward, backward, weight, retard_mask):
    less_space = jnp.einsum(
        "pkqc,pkor->orqc", less_part, forward, preferred_element_type=jnp.float32
    )
    more_space = jnp.einsum(
        "pkqc,pkor->orqc", more_part, forward, preferred_element_type=jnp.float32
    )
    less_re, less_im = (less_space[0], less_space[1])
    more_re, more_im = (more_space[0], more_space[1])
    square_re = less_re * less_re - less_im * less_im
    square_im = 2.0 * less_re * less_im
    sigma_less_re = -weight * (square_re * more_re + square_im * more_im)
    sigma_less_im = -weight * (square_im * more_re - square_re * more_im)
    other_re = more_re * more_re - more_im * more_im
    other_im = 2.0 * more_re * more_im
    sigma_more_re = -weight * (other_re * less_re + other_im * less_im)
    sigma_more_im = -weight * (other_im * less_re - other_re * less_im)
    sigma_less_space = jnp.stack([sigma_less_re, sigma_less_im]).astype(jnp.bfloat16)
    sigma_more_space = jnp.stack([sigma_more_re, sigma_more_im]).astype(jnp.bfloat16)
    less_mom = jnp.einsum(
        "orqc,orsk->skqc", sigma_less_space, backward, preferred_element_type=jnp.float32
    )
    more_mom = jnp.einsum(
        "orqc,orsk->skqc", sigma_more_space, backward, preferred_element_type=jnp.float32
    )
    sigma_ret = (retard_mask * (more_mom - less_mom)).astype(jnp.bfloat16)
    return (sigma_ret, less_mom.astype(jnp.bfloat16))


def complex_product(left_side, right_side):
    flipped = -left_side[1]
    real_part = jnp.einsum(
        "kts,ksc->ktc", left_side[0], right_side[0], preferred_element_type=jnp.float32
    )
    real_part = real_part + jnp.einsum(
        "kts,ksc->ktc", flipped, right_side[1], preferred_element_type=jnp.float32
    )
    imag_part = jnp.einsum(
        "kts,ksc->ktc", left_side[0], right_side[1], preferred_element_type=jnp.float32
    )
    imag_part = imag_part + jnp.einsum(
        "kts,ksc->ktc", left_side[1], right_side[0], preferred_element_type=jnp.float32
    )
    return jnp.stack([real_part, imag_part])


def collision_terms(sigma_ret, sigma_less, piece_less, piece_more):
    piece_rows = piece_less.shape[2]
    col_count = piece_less.shape[3]
    row_times = jnp.arange(piece_rows, dtype=jnp.int32)
    col_index = jnp.arange(col_count, dtype=jnp.int32)
    upper_mask = (row_times[:, None] <= col_index[None, :]).astype(jnp.float32)
    advanced = (
        -upper_mask * (piece_more.astype(jnp.float32) - piece_less.astype(jnp.float32))
    ).astype(jnp.bfloat16)
    return complex_product(sigma_ret, piece_less) + complex_product(sigma_less, advanced)


def on_device(lesser, greater, momentum_ids, window_start):
    part_count, local_k, row_count, col_count = lesser.shape
    groups = lax.axis_size("mom")
    sub_rows = row_count // groups
    forward, backward = transforms(momentum_ids)
    spread_less, spread_more = (
        lax.all_to_all(lesser, "mom", split_axis=2, concat_axis=1, tiled=True),
        lax.all_to_all(greater, "mom", split_axis=2, concat_axis=1, tiled=True),
    )
    row_first = lax.axis_index("trow") * row_count + lax.axis_index("mom") * sub_rows
    row_times = row_first + jnp.arange(sub_rows, dtype=jnp.int32)
    col_index = jnp.arange(col_count, dtype=jnp.int32)
    weight = drive(window_start, row_times)[:, None] * drive(window_start, col_index)[None, :]
    retard_mask = (row_times[:, None] >= col_index[None, :]).astype(jnp.float32)
    retarded, sigma_part = second_born(
        spread_less, spread_more, forward, backward, weight, retard_mask
    )
    sigma_ret, sigma_less = (
        lax.all_to_all(retarded, "mom", split_axis=1, concat_axis=2, tiled=True),
        lax.all_to_all(sigma_part, "mom", split_axis=1, concat_axis=2, tiled=True),
    )
    collected = collision_terms(
        sigma_ret,
        sigma_less,
        lax.all_gather(lesser, "trow", axis=2, tiled=True),
        lax.all_gather(greater, "trow", axis=2, tiled=True),
    )
    return (TIME_STEP * collected).astype(jnp.bfloat16)


def solution(mesh):
    return jax.shard_map(
        on_device,
        mesh=mesh,
        in_specs=(P(None, "mom", "trow", None), P(None, "mom", "trow", None), P(), P()),
        out_specs=P(None, "mom", "trow", None),
        check_vma=False,
    )
```

profile of v0, /device:TPU:7, one launch (start us, length us, event | category | flops | bytes accessed | tf_op | source)
XLA Modules:
  0.0 1022.7 jit_solution(16969149060503661734)
XLA Ops:
  7.3 13.2 %copy.19 = bf16[2,32,128,512]{3,1,0,2:T(8,128)(2,1)} copy(bf16[2,32,128,512]{3,2,1,0:T(8,128)(2,1)} %param.4) | data formatting | bytes 16777216 | tf_op args[0]
  20.4 6.1 all-to-all-start.1
  26.5 13.5 %copy.17 = bf16[2,32,128,512]{3,1,0,2:T(8,128)(2,1)} copy(bf16[2,32,128,512]{3,2,1,0:T(8,128)(2,1)} %param.5) | data formatting | bytes 16777216 | tf_op args[1]
  40.0 168.9 %all-to-all-done.1 = bf16[2,32,128,512]{3,1,0,2:T(8,128)(2,1)} async-done(((bf16[2,32,128,512]{3,1,0,2:T(8,128)(2,1)}), bf16[2,32,128,512]{3,1,0,2:T(8,128)(2,1)}, u32[]{:S(2)}, u32[]{:S(2)}) %all-to-all-start.1) | async-done | bytes 8388640 | tf_op jit(solution)/shard_map/all_to_all | solution.py:110
  208.9 4.9 all-to-all-start
  218.3 9.7 copy.20
  228.0 167.9 %all-to-all-done = bf16[2,32,128,512]{3,1,0,2:T(8,128)(2,1)} async-done(((bf16[2,32,128,512]{3,1,0,2:T(8,128)(2,1)}), bf16[2,32,128,512]{3,1,0,2:T(8,128)(2,1)}, u32[]{:S(2)}, u32[]{:S(2)}) %all-to-all-start) | async-done | bytes 8388640 | tf_op jit(solution)/shard_map/all_to_all | solution.py:111
  396.0 8.3 copy.18
  404.3 7.1 convolution_bitcast_fusion
  411.4 8.4 convolution_bitcast_fusion.1
  419.9 13.0 %multiply_convert_fusion.4 = (bf16[1,256,16,512]{3,1,2,0:T(8,128)(2,1)}, bf16[1,256,16,512]{3,1,2,0:T(8,128)(2,1)S(1)}, bf16[1,256,16,512]{3,1,2,0:T(8,128)(2,1)S(1)}, bf16[1,256,16,512]{3,1,2,0:T(8,128)(2,1)}) fusion(f32[2,256,16,512]{3,1,2,0:T(8,128)S(1)} %convolution_bitcast_fusion, f32[16,512]{1,0:T(8,128)S(1)} %multiply_negate_fusion.4, ...), kind=kLoop, calls=%fused_computation.39 | loop fusion | flops 62914560 | bytes 50364416 | tf_op jit(solution)/shard_map/convert.2
  432.8 10.9 %bitcast_convert_fusion = (bf16[2,256,16,512]{3,1,2,0:T(8,128)(2,1)}, f32[2,256,16,512,1]{3,1,4,2,0:T(8,128)}) fusion(bf16[1,256,16,512]{3,1,2,0:T(8,128)(2,1)S(1)} %get-tuple-element.6, bf16[1,256,16,512]{3,1,2,0:T(8,128)(2,1)S(1)} %get-tuple-element.7, bf16[1,256,2,256]{1,3,2,0:T(8,128)(2,1)S(1)} %get-tuple-element.16, ...), kind=kOutput, calls=%fused_computation.8 | convolution fusion | flops 4303618048 | bytes 34078720 | tf_op jit(solution)/shard_map/orqc,orsk->skqc/dot_general | solution.py:65
  443.7 13.2 %fusion.3 = bf16[2,256,16,512]{3,1,2,0:T(8,128)(2,1)} fusion(f32[2,256,16,512,1]{3,1,4,2,0:T(8,128)} %get-tuple-element.26, f32[16,512]{1,0:T(8,128)S(1)} %fusion.51, bf16[1,256,16,512]{3,1,2,0:T(8,128)(2,1)} %get-tuple-element.8, bf16[1,256,16,512]{3,1,2,0:T(8,128)(2,1)} %get-tuple-element.5, bf16[1,256,2,256]{1,3,2,0:T(8,128)(2,1)S(1)} %get-tuple-element.16, ...), kind=kOutput, calls=%fused_computation.11 | convolution fusion | flops 4312006656 | bytes 34111488 | tf_op jit(solution)/shard_map/orqc,orsk->skqc/dot_general | solution.py:68
  457.0 11.4 %copy.25 = bf16[2,256,16,512]{3,2,0,1:T(8,128)(2,1)} copy(bf16[2,256,16,512]{3,1,2,0:T(8,128)(2,1)} %fusion.3) | data formatting | bytes 16777216 | tf_op jit(solution)/shard_map/convert_element_type | solution.py:71
  468.4 4.9 all-to-all-start.2
  473.3 11.4 %copy.27 = bf16[2,256,16,512]{3,2,0,1:T(8,128)(2,1)} copy(bf16[2,256,16,512]{3,1,2,0:T(8,128)(2,1)} %get-tuple-element.25) | data formatting | bytes 16777216 | tf_op jit(solution)/shard_map/convert_element_type | solution.py:72
  484.7 170.8 %all-to-all-done.2 = bf16[2,256,16,512]{3,2,0,1:T(8,128)(2,1)} async-done(((bf16[2,256,16,512]{3,2,0,1:T(8,128)(2,1)}), bf16[2,256,16,512]{3,2,0,1:T(8,128)(2,1)}, u32[]{:S(2)}, u32[]{:S(2)}) %all-to-all-start.2) | async-done | bytes 8388640 | tf_op jit(solution)/shard_map/all_to_all | solution.py:122
  655.5 5.1 all-to-all-start.3
  660.7 8.2 copy.61
  669.0 173.9 %all-to-all-done.3 = bf16[2,256,16,512]{3,2,0,1:T(8,128)(2,1)} async-done(((bf16[2,256,16,512]{3,2,0,1:T(8,128)(2,1)}), bf16[2,256,16,512]{3,2,0,1:T(8,128)(2,1)}, u32[]{:S(2)}, u32[]{:S(2)}) %all-to-all-start.3) | async-done | bytes 8388640 | tf_op jit(solution)/shard_map/all_to_all | solution.py:123
  842.9 8.1 copy.60
  851.0 7.2 fusion.73
  863.4 33.4 %multiply_convert_fusion = bf16[2,32,512,512]{3,2,1,0:T(8,128)(2,1)} fusion(bf16[2,32,512,512]{3,2,1,0:T(8,128)(2,1)} %all-gather.3.cloned.1.call-done, bf16[2,32,512,512]{3,2,1,0:T(8,128)(2,1)} %all-gather.5.cloned.1.call-done, f32[512,512]{1,0:T(8,128)S(1)} %convert_negate_fusion), kind=kLoop, calls=%fused_computation | loop fusion | flops 83886080 | bytes 101711872 | tf_op jit(solution)/shard_map/convert_element_type | solution.py:100
  896.8 12.9 %fusion.8 = f32[32,128,512]{2,1,0:T(8,128)} fusion(bf16[32,128,512]{2,1,0:T(8,128)(2,1)} %bitcast.121, bf16[2,32,512,512]{3,2,1,0:T(8,128)(2,1)} %multiply_convert_fusion), kind=kOutput, calls=%fused_computation.16 | convolution fusion | flops 2147483648 | bytes 29360128 | tf_op jit(solution)/shard_map/kts,ksc->ktc/dot_general | solution.py:86
  909.7 11.4 %fusion.9 = f32[32,128,512]{2,1,0:T(8,128)} fusion(bf16[32,128,512]{2,1,0:T(8,128)(2,1)S(1)} %bitcast.123, bf16[2,32,512,512]{3,2,1,0:T(8,128)(2,1)} %multiply_convert_fusion), kind=kOutput, calls=%fused_computation.17 | convolution fusion | flops 2147483648 | bytes 29360128 | tf_op jit(solution)/shard_map/kts,ksc->ktc/dot_general | solution.py:77
  921.1 13.1 %add_bitcast_fusion = f32[1,32,128,512]{3,2,1,0:T(8,128)} fusion(f32[32,128,512]{2,1,0:T(8,128)} %fusion.8, bf16[32,128,512]{2,1,0:T(8,128)(2,1)S(1)} %bitcast.124, bf16[2,32,512,512]{3,2,1,0:T(8,128)(2,1)} %multiply_convert_fusion), kind=kOutput, calls=%fused_computation.30 | convolution fusion | flops 2149580800 | bytes 37748736 | tf_op jit(solution)/shard_map/kts,ksc->ktc/dot_general | solution.py:83
  934.3 14.4 %add_bitcast_fusion.1 = f32[1,32,128,512]{3,2,1,0:T(8,128)} fusion(f32[32,128,512]{2,1,0:T(8,128)} %fusion.9, bf16[2,32,512,512]{3,2,1,0:T(8,128)(2,1)} %multiply_convert_fusion, bf16[32,128,512]{2,1,0:T(8,128)(2,1)} %bitcast.122), kind=kOutput, calls=%fused_computation.31 | convolution fusion | flops 2151677952 | bytes 37748736 | tf_op jit(solution)/shard_map/kts,ksc->ktc/dot_general | solution.py:80
  948.7 12.9 %fusion.4 = f32[32,128,512]{2,1,0:T(8,128)} fusion(bf16[32,128,512]{2,1,0:T(8,128)(2,1)} %bitcast.117, bf16[2,32,512,512]{3,2,1,0:T(8,128)(2,1)} %all-gather.3.cloned.1.call-done), kind=kOutput, calls=%fused_computation.12 | convolution fusion | flops 2147483648 | bytes 29360128 | tf_op jit(solution)/shard_map/kts,ksc->ktc/dot_general | solution.py:86
  961.6 11.4 %fusion.5 = f32[32,128,512]{2,1,0:T(8,128)} fusion(bf16[32,128,512]{2,1,0:T(8,128)(2,1)S(1)} %bitcast.119, bf16[2,32,512,512]{3,2,1,0:T(8,128)(2,1)} %all-gather.3.cloned.1.call-done), kind=kOutput, calls=%fused_computation.13 | convolution fusion | flops 2147483648 | bytes 29360128 | tf_op jit(solution)/shard_map/kts,ksc->ktc/dot_general | solution.py:77
  973.1 13.1 %add_bitcast_fusion.2 = f32[1,32,128,512]{3,2,1,0:T(8,128)} fusion(f32[32,128,512]{2,1,0:T(8,128)} %fusion.4, bf16[32,128,512]{2,1,0:T(8,128)(2,1)S(1)} %bitcast.120, bf16[2,32,512,512]{3,2,1,0:T(8,128)(2,1)} %all-gather.3.cloned.1.call-done), kind=kOutput, calls=%fused_computation.32 | convolution fusion | flops 2149580800 | bytes 37748736 | tf_op jit(solution)/shard_map/kts,ksc->ktc/dot_general | solution.py:83
  986.1 14.3 %add_bitcast_fusion.3 = f32[1,32,128,512]{3,2,1,0:T(8,128)} fusion(f32[32,128,512]{2,1,0:T(8,128)} %fusion.5, bf16[2,32,512,512]{3,2,1,0:T(8,128)(2,1)} %all-gather.3.cloned.1.call-done, bf16[32,128,512]{2,1,0:T(8,128)(2,1)} %bitcast.118), kind=kOutput, calls=%fused_computation.33 | convolution fusion | flops 2151677952 | bytes 37748736 | tf_op jit(solution)/shard_map/kts,ksc->ktc/dot_general | solution.py:80
  1000.4 15.0 %fusion.1 = bf16[2,32,128,512]{3,2,1,0:T(8,128)(2,1)} fusion(f32[1,32,128,512]{3,2,1,0:T(8,128)} %add_bitcast_fusion.2, f32[1,32,128,512]{3,2,1,0:T(8,128)} %add_bitcast_fusion.3, f32[1,32,128,512]{3,2,1,0:T(8,128)} %add_bitcast_fusion, f32[1,32,128,512]{3,2,1,0:T(8,128)} %add_bitcast_fusion.1), kind=kLoop, calls=%fused_computation.7 | loop fusion | flops 20971520 | bytes 41943040 | tf_op jit(solution)/shard_map/convert_element_type | solution.py:131
  (28 shorter events, 9.8 us)
Async XLA Ops:
  6.5 856.9 %all-gather.3.cloned.1.call-start = ((), (), s32[]{:S(2)}) async-start(), calls=%async_computation.4 | async-start | bytes 41943040 | tf_op jit(solution)/shard_map/all_gather | solution.py:128
  20.4 188.5 %all-to-all-start.1 = ((bf16[2,32,128,512]{3,1,0,2:T(8,128)(2,1)}), bf16[2,32,128,512]{3,1,0,2:T(8,128)(2,1)}, u32[]{:S(2)}, u32[]{:S(2)}) async-start(bf16[2,32,128,512]{3,1,0,2:T(8,128)(2,1)} %copy.19), calls=%async_computation.1 | async-start | bytes 16777216 | tf_op jit(solution)/shard_map/all_to_all | solution.py:110
  208.9 187.0 %all-to-all-start = ((bf16[2,32,128,512]{3,1,0,2:T(8,128)(2,1)}), bf16[2,32,128,512]{3,1,0,2:T(8,128)(2,1)}, u32[]{:S(2)}, u32[]{:S(2)}) async-start(bf16[2,32,128,512]{3,1,0,2:T(8,128)(2,1)} %copy.17), calls=%async_computation | async-start | bytes 16777216 | tf_op jit(solution)/shard_map/all_to_all | solution.py:111
  213.8 1.6 copy-start.4
  213.8 649.6 %all-gather.5.cloned.1.call-start = ((), (), s32[]{:S(2)}) async-start(), calls=%async_computation.5 | async-start | bytes 41943040 | tf_op jit(solution)/shard_map/all_gather | solution.py:129
  404.3 7.1 copy-start.3
  468.4 187.1 %all-to-all-start.2 = ((bf16[2,256,16,512]{3,2,0,1:T(8,128)(2,1)}), bf16[2,256,16,512]{3,2,0,1:T(8,128)(2,1)}, u32[]{:S(2)}, u32[]{:S(2)}) async-start(bf16[2,256,16,512]{3,2,0,1:T(8,128)(2,1)} %copy.25), calls=%async_computation.2 | async-start | bytes 16777216 | tf_op jit(solution)/shard_map/all_to_all | solution.py:122
  655.5 187.4 %all-to-all-start.3 = ((bf16[2,256,16,512]{3,2,0,1:T(8,128)(2,1)}), bf16[2,256,16,512]{3,2,0,1:T(8,128)(2,1)}, u32[]{:S(2)}, u32[]{:S(2)}) async-start(bf16[2,256,16,512]{3,2,0,1:T(8,128)(2,1)} %copy.27), calls=%async_computation.3 | async-start | bytes 16777216 | tf_op jit(solution)/shard_map/all_to_all | solution.py:123
  851.0 8.8 copy-start.2
  896.8 12.9 %copy-start.1 = (bf16[1,32,8,16,512]{4,3,2,1,0:T(8,128)(2,1)S(1)}, bf16[1,32,8,16,512]{4,3,2,1,0:T(8,128)(2,1)}, u32[]{:S(2)}) copy-start(bf16[1,32,8,16,512]{4,3,2,1,0:T(8,128)(2,1)} %get-tuple-element.9) | copy-start | bytes 12582916
  948.7 12.9 %copy-start = (bf16[1,32,8,16,512]{4,3,2,1,0:T(8,128)(2,1)S(1)}, bf16[1,32,8,16,512]{4,3,2,1,0:T(8,128)(2,1)}, u32[]{:S(2)}) copy-start(bf16[1,32,8,16,512]{4,3,2,1,0:T(8,128)(2,1)} %get-tuple-element.11) | copy-start | bytes 12582916
Sparse Core Ops, SparseCore 0:
  8.9 202.2 all-gather.2
  216.3 203.1 all-gather.4
where the time goes:
time: 1030 us; the launch traced here: 1020 us
  waiting for transfers between devices  683 us (66%)
  matrix products  143 us (14%)
  local copies, waits for them, and re-layouts  96.2 us (9%)
  other arithmetic  64.5 us (6%)
  starting transfers between devices  21.5 us (2%)
  between operations  14.6 us (1%)
    all_to_all x1, waiting for transfers between devices, on_device(): lax.all_to_all(sigma_part, 'mom', split_axis=1, concat_axis=2, tiled=True)  174 us
    all_to_all x1, waiting for transfers between devices, on_device(): lax.all_to_all(retarded, 'mom', split_axis=1, concat_axis=2, tiled=True)  171 us
    all_to_all x1, waiting for transfers between devices, on_device(): lax.all_to_all(lesser, 'mom', split_axis=2, concat_axis=1, tiled=True)  169 us
    all_to_all x1, waiting for transfers between devices, on_device(): lax.all_to_all(greater, 'mom', split_axis=2, concat_axis=1, tiled=True)  168 us
    convert_element_type x1, other arithmetic, collision_terms(): advanced = (-upper_mask * (piece_more.astype(jnp.float32) - piece_less.as...  33.4 us
    dot_general x2, matrix products, complex_product(): jnp.einsum('kts,ksc->ktc', flipped, right_side[1], preferred_element_type...  28.7 us
    unnamed x12, local copies, waits for them, and re-layouts  28.2 us
    dot_general x2, matrix products, complex_product(): jnp.einsum('kts,ksc->ktc', left_side[0], right_side[1], preferred_element...  26.2 us
  transfers between devices with their start and end apart: 6, of which 4 were waited for; matrix products, arithmetic and copies ran while one was open for 15% of the time, Pallas kernels for 0%

commit v1 on v0

v1 whole, which is shorter than its diff:
```python
import functools

import jax
import jax.numpy as jnp
import numpy as np
from jax import lax
from jax.experimental import pallas as pl
from jax.experimental.pallas import tpu as pltpu
from jax.sharding import PartitionSpec as P

LX = 16
LY = 16
DRIVE = 128


U_BASE = 4.0
TIME_STEP = 0.02

COLUMN_PARTS = 2
VMEM_BYTES = 56 * 1024 * 1024


def lattice_tables(momentum_ids):
    momenta = momentum_ids.shape[0]
    wave_x = momentum_ids // LY
    wave_y = momentum_ids % LY
    sites = jnp.arange(momenta, dtype=jnp.int32)
    site_x = sites // LY
    site_y = sites % LY
    phase = (
        wave_x[:, None] * site_x[None, :] % LX * LY + wave_y[:, None] * site_y[None, :] % LY * LX
    )
    angle = 2.0 * jnp.pi / momenta * (phase % momenta).astype(jnp.float32)
    return (jnp.cos(angle), jnp.sin(angle), momenta)


def transforms(momentum_ids, groups):
    cos_table, sin_table, momenta = lattice_tables(momentum_ids)
    local_k = momenta // groups
    forward = jnp.stack(
        [jnp.stack([cos_table, sin_table], 1), jnp.stack([-sin_table, cos_table], 1)], 0
    )
    forward = (forward / momenta).astype(jnp.bfloat16)
    forward = forward.reshape(2, groups, local_k, 2, momenta).transpose(3, 4, 1, 0, 2)
    backward = jnp.stack(
        [jnp.stack([cos_table.T, -sin_table.T], 1), jnp.stack([sin_table.T, cos_table.T], 1)], 0
    ).astype(jnp.bfloat16)
    backward = backward.reshape(2, momenta, 2, groups, local_k).transpose(3, 2, 4, 0, 1)
    return (
        forward.reshape(2 * momenta, 2 * momenta),
        backward.reshape(2 * momenta, 2 * momenta),
    )


def drive(window_start, row_times):
    phase = ((window_start[0] + row_times) % DRIVE).astype(jnp.float32)
    return U_BASE * (1.0 + 0.5 * jnp.sin(2.0 * jnp.pi / DRIVE * phase))


def born_kernel(x_ref, forward_ref, backward_ref, weight_ref, mask_ref, out_ref):
    groups, _, _, depth, width = x_ref.shape
    half = groups * depth // 2
    table = forward_ref[...]
    weight = -weight_ref[0]
    less = jnp.dot(
        table, x_ref[:, 0, 0].reshape(groups * depth, width), preferred_element_type=jnp.float32
    )
    more = jnp.dot(
        table, x_ref[:, 1, 0].reshape(groups * depth, width), preferred_element_type=jnp.float32
    )
    less_re, less_im = (less[:half], less[half:])
    more_re, more_im = (more[:half], more[half:])
    square_re = less_re * less_re - less_im * less_im
    square_im = 2.0 * less_re * less_im
    sigma_less = jnp.concatenate(
        [
            (weight * (square_re * more_re + square_im * more_im)).astype(jnp.bfloat16),
            (weight * (square_im * more_re - square_re * more_im)).astype(jnp.bfloat16),
        ],
        axis=0,
    )
    other_re = more_re * more_re - more_im * more_im
    other_im = 2.0 * more_re * more_im
    sigma_more = jnp.concatenate(
        [
            (weight * (other_re * less_re + other_im * less_im)).astype(jnp.bfloat16),
            (weight * (other_im * less_re - other_re * less_im)).astype(jnp.bfloat16),
        ],
        axis=0,
    )
    back = backward_ref[...]
    less_mom = jnp.dot(back, sigma_less, preferred_element_type=jnp.float32)
    more_mom = jnp.dot(back, sigma_more, preferred_element_type=jnp.float32)
    ret = (mask_ref[0] * (more_mom - less_mom)).astype(jnp.bfloat16)
    out_ref[:, 0, 0] = less_mom.astype(jnp.bfloat16).reshape(groups, depth, width)
    out_ref[:, 1, 0] = ret.reshape(groups, depth, width)


def born(spread, forward, backward, weight, mask):
    groups, _, sub_rows, depth, width = spread.shape
    size = groups * depth
    return pl.pallas_call(
        born_kernel,
        grid=(sub_rows,),
        in_specs=[
            pl.BlockSpec((groups, 2, 1, depth, width), lambda i: (0, 0, i, 0, 0)),
            pl.BlockSpec((size, size), lambda i: (0, 0)),
            pl.BlockSpec((size, size), lambda i: (0, 0)),
            pl.BlockSpec((1, 1, width), lambda i: (i, 0, 0)),
            pl.BlockSpec((1, 1, width), lambda i: (i, 0, 0)),
        ],
        out_specs=pl.BlockSpec((groups, 2, 1, depth, width), lambda i: (0, 0, i, 0, 0)),
        out_shape=jax.ShapeDtypeStruct(spread.shape, jnp.bfloat16),
        compiler_params=pltpu.CompilerParams(vmem_limit_bytes=VMEM_BYTES),
        cost_estimate=pl.CostEstimate(
            flops=8 * size * size * sub_rows * width,
            bytes_accessed=4 * spread.size,
            transcendentals=0,
        ),
        name="born",
    )(spread, forward, backward, weight, mask)


def collide_kernel(first_col, last, sigma_ref, less_ref, more_ref, *refs):
    total_ref, out_ref = (None, refs[0]) if len(refs) == 1 else refs
    rows, cols = out_ref.shape[2:]
    steps = less_ref.shape[2]

    def left(kind, part):
        return sigma_ref[:, kind, part, 0].reshape(rows, steps)

    less_re, less_im = (less_ref[0, 0], less_ref[1, 0])
    step_index = first_col + lax.broadcasted_iota(jnp.int32, (steps, cols), 0)
    upper = step_index <= lax.broadcasted_iota(jnp.int32, (steps, cols), 1)

    def advanced(part):
        gap = less_ref[part, 0].astype(jnp.float32) - more_ref[part, 0].astype(jnp.float32)
        return jnp.where(upper, gap, 0.0).astype(jnp.bfloat16)

    right = jnp.concatenate([less_re, less_im, advanced(0), advanced(1)], axis=0)
    lesser_re, lesser_im = (left(0, 0), left(0, 1))
    ret_re, ret_im = (left(1, 0), left(1, 1))
    lefts = jnp.concatenate(
        [
            jnp.concatenate([ret_re, -ret_im, lesser_re, -lesser_im], axis=1),
            jnp.concatenate([ret_im, ret_re, lesser_im, lesser_re], axis=1),
        ],
        axis=0,
    )
    product = jnp.dot(lefts, right, preferred_element_type=jnp.float32)
    for part in range(2):
        value = product[part * rows : (part + 1) * rows]
        if total_ref is not None:
            value = total_ref[part, 0] + value
        if last:
            value = TIME_STEP * value
        out_ref[part, 0] = value.astype(out_ref.dtype)


def collide(sigma, less_all, more_all, total, first_col, last):
    groups, _, _, local_k, sub_rows, width = sigma.shape
    rows, cols = (groups * sub_rows, less_all.shape[3])
    sigma_spec = pl.BlockSpec(
        (groups, 2, 2, 1, sub_rows, width), lambda k: (0, 0, 0, k, 0, 0)
    )
    piece_spec = pl.BlockSpec((2, 1, width, cols), lambda k: (0, k, first_col // width, 0))
    out_spec = pl.BlockSpec((2, 1, rows, cols), lambda k: (0, k, 0, 0))
    totals = () if total is None else (total,)
    kind = jnp.bfloat16 if last else jnp.float32
    return pl.pallas_call(
        functools.partial(collide_kernel, first_col, last),
        grid=(local_k,),
        in_specs=[sigma_spec, piece_spec, piece_spec] + [out_spec] * len(totals),
        out_specs=out_spec,
        out_shape=jax.ShapeDtypeStruct((2, local_k, rows, cols), kind),
        compiler_params=pltpu.CompilerParams(vmem_limit_bytes=VMEM_BYTES),
        cost_estimate=pl.CostEstimate(
            flops=16 * local_k * rows * width * cols,
            bytes_accessed=2 * sigma.size + 8 * local_k * width * cols + 12 * local_k * rows * cols,
            transcendentals=0,
        ),
        name="collide",
    )(sigma, less_all, more_all, *totals)


def swap_groups(part):
    return lax.all_to_all(part, "mom", split_axis=0, concat_axis=0, tiled=True)


def on_device(lesser, greater, momentum_ids, window_start):
    _, local_k, row_count, col_count = lesser.shape
    groups = lax.axis_size("mom")
    sub_rows = row_count // groups
    width = col_count // COLUMN_PARTS
    row_first = lax.axis_index("trow") * row_count + lax.axis_index("mom") * sub_rows
    row_times = row_first + jnp.arange(sub_rows, dtype=jnp.int32)

    spreads = []
    for part in range(COLUMN_PARTS):
        both = jnp.stack([lesser, greater])[..., part * width : (part + 1) * width]
        both = both.reshape(2, 2, local_k, groups, sub_rows, width).transpose(3, 0, 4, 1, 2, 5)
        spreads.append(swap_groups(both.reshape(groups, 2, sub_rows, 2 * local_k, width)))

    less_all = lax.all_gather(lesser, "trow", axis=2, tiled=True)
    more_all = lax.all_gather(greater, "trow", axis=2, tiled=True)
    forward, backward = transforms(momentum_ids, groups)
    row_drive = drive(window_start, row_times)

    sigmas = []
    for part in range(COLUMN_PARTS):
        col_index = part * width + jnp.arange(width, dtype=jnp.int32)
        weight = row_drive[:, None] * drive(window_start, col_index)[None, :]
        mask = (row_times[:, None] >= col_index[None, :]).astype(jnp.float32)
        sigma = born(spreads[part], forward, backward, weight[:, None], mask[:, None])
        sigma = sigma.transpose(0, 1, 3, 2, 4)
        sigmas.append(swap_groups(sigma))

    total = None
    for part in range(COLUMN_PARTS):
        sigma = sigmas[part].reshape(groups, 2, 2, local_k, sub_rows, width)
        if sub_rows % 16:
            sigma = sigma.transpose(1, 2, 3, 0, 4, 5).reshape(
                1, 2, 2, local_k, groups * sub_rows, width
            )
        total = collide(
            sigma, less_all, more_all, total, part * width, part == COLUMN_PARTS - 1
        )
    return total


def solution(mesh):
    return jax.shard_map(
        on_device,
        mesh=mesh,
        in_specs=(P(None, "mom", "trow", None), P(None, "mom", "trow", None), P(), P()),
        out_specs=P(None, "mom", "trow", None),
        check_vma=False,
    )
```

time: 1030 us -> 881 us (0.86)
  matrix products: 143 us -> 0 us
  Pallas kernels: 0 us -> 111 us
  other arithmetic: 64.5 us -> 18.1 us
  local copies, waits for them, and re-layouts: 96.2 us -> 55.1 us
  waiting for transfers between devices: 683 us -> 657 us
    dot_general x12 -> x0, matrix products: 143 us -> none  [the longest x2 28.7 us: complex_product(): jnp.einsum('kts,ksc->ktc', flipped, right_side[1], preferred_element_type...]
    pallas_call x0 -> x4, Pallas kernels: none -> 111 us  [the longest x2 70.2 us: collide(): pl.pallas_call(functools.partial(collide_kernel, first_col, last), grid=(...]
    convert_element_type x3 -> x1, other arithmetic: 48.5 us -> 0.7 us  [on_device(): mask = (row_times[:, None] >= col_index[None, :]).astype(jnp.float32)]
    reshape x0 -> x3, local copies, waits for them, and re-layouts: none -> 27.9 us  [the longest x2 26.8 us: on_device(): both.reshape(2, 2, local_k, groups, sub_rows, width)]
    unnamed x12 -> x4, local copies, waits for them, and re-layouts: 28.2 us -> 0.98 us
    all_to_all x4, waiting for transfers between devices: 682 us -> 655 us  [swap_groups(): return lax.all_to_all(part, 'mom', split_axis=0, concat_axis=0, tiled=True)]
    convert_element_type x2 -> x0, local copies, waits for them, and re-layouts: 22.8 us -> none  [the longest x1 11.4 us: second_born(): sigma_ret = (retard_mask * (more_mom - less_mom)).astype(jnp.bfloat16)]
    slice x2 -> x0, local copies, waits for them, and re-layouts: 10.9 us -> none  [complex_product(): left_side[0]]
  transfers between devices with their start and end apart: 6 -> 6, of which waited for: 4 -> 4; matrix products, arithmetic and copies ran while one was open for 15% -> 8% of each run, Pallas kernels for 0% -> 5%
where the time goes in v1:
time: 881 us; the launch traced here: 876 us
  waiting for transfers between devices  657 us (75%)
  Pallas kernels  111 us (13%)
  local copies, waits for them, and re-layouts  55.1 us (6%)
  starting transfers between devices  20.8 us (2%)
  other arithmetic  18.1 us (2%)
  between operations  14.2 us (2%)
    all_to_all x4, waiting for transfers between devices, swap_groups(): return lax.all_to_all(part, 'mom', split_axis=0, concat_axis=0, tiled=True)  655 us
    pallas_call x2, Pallas kernels, collide(): pl.pallas_call(functools.partial(collide_kernel, first_col, last), grid=(...  70.2 us
    pallas_call x2, Pallas kernels, born(): pl.pallas_call(born_kernel, grid=(sub_rows,), in_specs=[pl.BlockSpec((gro...  40.6 us
    reshape x2, local copies, waits for them, and re-layouts, on_device(): both.reshape(2, 2, local_k, groups, sub_rows, width)  26.8 us
    all_to_all x2, local copies, waits for them, and re-layouts, swap_groups(): return lax.all_to_all(part, 'mom', split_axis=0, concat_axis=0, tiled=True)  25 us
    all_to_all x4, starting transfers between devices, swap_groups(): return lax.all_to_all(part, 'mom', split_axis=0, concat_axis=0, tiled=True)  20.8 us
  transfers between devices with their start and end apart: 6, of which 4 were waited for; matrix products, arithmetic and copies ran while one was open for 8% of the time, Pallas kernels for 5%

profile of v1, /device:TPU:7, one launch (start us, length us, event | category | flops | bytes accessed | tf_op | source)
XLA Modules:
  0.0 875.8 jit_solution(11858586281865357606)
XLA Ops:
  6.5 0.7 all-gather.3.cloned.1.call-update
  7.3 13.6 %pad_maximum_fusion = (bf16[2,2,32,128,256]{4,3,2,1,0:T(8,128)(2,1)}, bf16[2,2,32,128,256]{4,3,2,1,0:T(8,128)(2,1)}) fusion(bf16[1,2,32,128,512]{4,3,2,1,0:T(8,128)(2,1)} %bitcast.33, bf16[1,2,32,128,512]{4,3,2,1,0:T(8,128)(2,1)} %bitcast.32), kind=kLoop, calls=%fused_computation.3 | loop fusion | flops 33554432 | bytes 33554432 | tf_op jit(solution)/shard_map/stack | solution.py:200
  20.8 15.4 %copy.15 = bf16[2,2,32,8,16,256]{5,2,1,4,0,3:T(8,128)(2,1)} copy(bf16[2,2,32,8,16,256]{5,4,3,2,1,0:T(8,128)(2,1)} %bitcast.35) | data formatting | bytes 16777216 | tf_op jit(solution)/shard_map/reshape | solution.py:201
  36.2 5.5 all-to-all-start
  41.7 0.7 all-gather.5.cloned.1.call-update
  42.5 11.4 %copy.21 = bf16[2,2,32,8,16,256]{5,2,1,4,0,3:T(8,128)(2,1)} copy(bf16[2,2,32,8,16,256]{5,4,3,2,1,0:T(8,128)(2,1)} %bitcast.34) | data formatting | bytes 16777216 | tf_op jit(solution)/shard_map/reshape | solution.py:201
  53.9 170.3 %all-to-all-done.x_ref = bf16[8,2,16,64,256]{4,3,2,1,0:T(8,128)(2,1)} async-done(((bf16[8,2,16,64,256]{4,3,2,1,0:T(8,128)(2,1)}), bf16[8,2,16,64,256]{4,3,2,1,0:T(8,128)(2,1)}, u32[]{:S(2)}, u32[]{:S(2)}) %all-to-all-start) | async-done | bytes 8388640 | tf_op jit(solution)/shard_map/all_to_all | solution.py:187
  224.2 5.5 all-to-all-start.2
  230.3 0.1 mul.285
  230.4 0.1 mul.289
  230.5 1.5 negate_convert_fusion
  232.0 0.5 copy.17
  232.6 0.9 copy.27
  233.5 1.3 fusion.19
  234.8 0.1 fusion.2
  234.9 0.5 copy.16
  235.5 0.1 copy.26
  235.5 1.1 copy.19.forward_ref
  236.7 0.1 fusion.29
  236.7 0.7 compare_convert_fusion
  237.4 0.7 broadcast_multiply_fusion
  238.1 20.4 %born.2 = bf16[8,2,16,64,256]{4,3,2,1,0:T(8,128)(2,1)} custom-call(bf16[8,2,16,64,256]{4,3,2,1,0:T(8,128)(2,1)} %all-to-all-done.x_ref, bf16[512,512]{1,0:T(8,128)(2,1)} %copy.19.forward_ref, bf16[512,512]{1,0:T(8,128)(2,1)} %bitcast.42, f32[16,1,256]{2,1,0:T(1,128)} %get-tuple-element.18.weight_ref, f32[16,1,256]{2,1,0:T(1,128)} %get-tuple-element.16.mask_ref), custom_call_target="tpu_custom_call" | custom-call | flops 8589934592 | bytes 16777216 | tf_op jit(solution)/shard_map/born/pallas_call | solution.py:102
  258.5 153.5 %all-to-all-done.2.x_ref = bf16[8,2,16,64,256]{4,3,2,1,0:T(8,128)(2,1)} async-done(((bf16[8,2,16,64,256]{4,3,2,1,0:T(8,128)(2,1)}), bf16[8,2,16,64,256]{4,3,2,1,0:T(8,128)(2,1)}, u32[]{:S(2)}, u32[]{:S(2)}) %all-to-all-start.2) | async-done | bytes 8388640 | tf_op jit(solution)/shard_map/all_to_all | solution.py:187
  412.0 4.9 all-to-all-start.1
  417.0 20.2 %born.3 = bf16[8,2,16,64,256]{4,3,2,1,0:T(8,128)(2,1)} custom-call(bf16[8,2,16,64,256]{4,3,2,1,0:T(8,128)(2,1)} %all-to-all-done.2.x_ref, bf16[512,512]{1,0:T(8,128)(2,1)} %copy.19.forward_ref, bf16[512,512]{1,0:T(8,128)(2,1)} %bitcast.43, f32[16,1,256]{2,1,0:T(1,128)} %get-tuple-element.17.weight_ref, f32[16,1,256]{2,1,0:T(1,128)} %get-tuple-element.15.mask_ref), custom_call_target="tpu_custom_call" | custom-call | flops 8589934592 | bytes 16777216 | tf_op jit(solution)/shard_map/born/pallas_call | solution.py:102
  437.2 161.8 %all-to-all-done.1 = bf16[8,2,64,16,256]{4,2,3,1,0:T(8,128)(2,1)} async-done(((bf16[8,2,64,16,256]{4,2,3,1,0:T(8,128)(2,1)}), bf16[8,2,64,16,256]{4,2,3,1,0:T(8,128)(2,1)}, u32[]{:S(2)}, u32[]{:S(2)}) %all-to-all-start.1) | async-done | bytes 8388640 | tf_op jit(solution)/shard_map/all_to_all | solution.py:187
  599.0 4.9 all-to-all-start.3
  603.9 12.5 %copy.20 = bf16[8,2,64,16,256]{4,3,2,1,0:T(8,128)(2,1)} copy(bf16[8,2,64,16,256]{4,2,3,1,0:T(8,128)(2,1)} %all-to-all-done.1) | data formatting | bytes 16777216 | tf_op jit(solution)/shard_map/all_to_all | solution.py:187
  616.4 169.8 %all-to-all-done.3 = bf16[8,2,64,16,256]{4,2,3,1,0:T(8,128)(2,1)} async-done(((bf16[8,2,64,16,256]{4,2,3,1,0:T(8,128)(2,1)}), bf16[8,2,64,16,256]{4,2,3,1,0:T(8,128)(2,1)}, u32[]{:S(2)}, u32[]{:S(2)}) %all-to-all-start.3) | async-done | bytes 8388640 | tf_op jit(solution)/shard_map/all_to_all | solution.py:187
  786.1 12.5 %copy.24 = bf16[8,2,64,16,256]{4,3,2,1,0:T(8,128)(2,1)} copy(bf16[8,2,64,16,256]{4,2,3,1,0:T(8,128)(2,1)} %all-to-all-done.3) | data formatting | bytes 16777216 | tf_op jit(solution)/shard_map/all_to_all | solution.py:187
  798.7 35.1 %collide.2.refs_0_ = f32[2,32,128,512]{3,2,1,0:T(8,128)} custom-call(bf16[8,2,2,32,16,256]{5,4,3,2,1,0:T(8,128)(2,1)} %bitcast.36, bf16[2,32,512,512]{3,2,1,0:T(8,128)(2,1)} %all-gather.3.cloned.1.call-done.less_ref, bf16[2,32,512,512]{3,2,1,0:T(8,128)(2,1)} %all-gather.5.cloned.1.call-done.more_ref), custom_call_target="tpu_custom_call" | custom-call | flops 8589934592 | bytes 67108864 | tf_op jit(solution)/shard_map/collide/pallas_call | solution.py:170
  833.7 35.2 %collide.3 = bf16[2,32,128,512]{3,2,1,0:T(8,128)(2,1)} custom-call(bf16[8,2,2,32,16,256]{5,4,3,2,1,0:T(8,128)(2,1)} %bitcast.29, bf16[2,32,512,512]{3,2,1,0:T(8,128)(2,1)} %all-gather.3.cloned.1.call-done.less_ref, bf16[2,32,512,512]{3,2,1,0:T(8,128)(2,1)} %all-gather.5.cloned.1.call-done.more_ref, f32[2,32,128,512]{3,2,1,0:T(8,128)} %collide.2.refs_0_), custom_call_target="tpu_custom_call" | custom-call | flops 8589934592 | bytes 67108864 | tf_op jit(solution)/shard_map/collide/pallas_call | solution.py:170
  (12 shorter events, 0.1 us)
Async XLA Ops:
  6.5 792.2 %all-gather.3.cloned.1.call-start = ((), (), s32[]{:S(2)}) async-start(), calls=%async_computation.4 | async-start | bytes 41943040 | tf_op jit(solution)/shard_map/all_gather | solution.py:204
  36.2 187.9 %all-to-all-start = ((bf16[8,2,16,64,256]{4,3,2,1,0:T(8,128)(2,1)}), bf16[8,2,16,64,256]{4,3,2,1,0:T(8,128)(2,1)}, u32[]{:S(2)}, u32[]{:S(2)}) async-start(bf16[8,2,16,64,256]{4,3,2,1,0:T(8,128)(2,1)} %bitcast.31), calls=%async_computation | async-start | bytes 16777216 | tf_op jit(solution)/shard_map/all_to_all | solution.py:187
  41.7 757.0 %all-gather.5.cloned.1.call-start = ((), (), s32[]{:S(2)}) async-start(), calls=%async_computation.5 | async-start | bytes 41943040 | tf_op jit(solution)/shard_map/all_gather | solution.py:205
  224.2 6.1 copy-start
  224.2 187.9 %all-to-all-start.2 = ((bf16[8,2,16,64,256]{4,3,2,1,0:T(8,128)(2,1)}), bf16[8,2,16,64,256]{4,3,2,1,0:T(8,128)(2,1)}, u32[]{:S(2)}, u32[]{:S(2)}) async-start(bf16[8,2,16,64,256]{4,3,2,1,0:T(8,128)(2,1)} %bitcast.30), calls=%async_computation.2 | async-start | bytes 16777216 | tf_op jit(solution)/shard_map/all_to_all | solution.py:187
  412.0 187.0 %all-to-all-start.1 = ((bf16[8,2,64,16,256]{4,2,3,1,0:T(8,128)(2,1)}), bf16[8,2,64,16,256]{4,2,3,1,0:T(8,128)(2,1)}, u32[]{:S(2)}, u32[]{:S(2)}) async-start(bf16[8,2,64,16,256]{4,2,3,1,0:T(8,128)(2,1)} %bitcast.37), calls=%async_computation.1 | async-start | bytes 16777216 | tf_op jit(solution)/shard_map/all_to_all | solution.py:187
  599.0 187.1 %all-to-all-start.3 = ((bf16[8,2,64,16,256]{4,2,3,1,0:T(8,128)(2,1)}), bf16[8,2,64,16,256]{4,2,3,1,0:T(8,128)(2,1)}, u32[]{:S(2)}, u32[]{:S(2)}) async-start(bf16[8,2,64,16,256]{4,2,3,1,0:T(8,128)(2,1)} %bitcast.38), calls=%async_computation.3 | async-start | bytes 16777216 | tf_op jit(solution)/shard_map/all_to_all | solution.py:187
Sparse Core Ops, SparseCore 0:
  8.9 202.2 all-gather.2
  212.8 201.5 all-gather.4

commit v2 on v1

v2 whole, which is shorter than its diff:
```python
import functools

import jax
import jax.numpy as jnp
from jax import lax
from jax.experimental import pallas as pl
from jax.experimental.pallas import tpu as pltpu
from jax.sharding import PartitionSpec as P

LX = 16
LY = 16
DRIVE = 128


U_BASE = 4.0
TIME_STEP = 0.02

MOMENTA_BLOCK = 2
VMEM_BYTES = 56 * 1024 * 1024


def lattice_tables(momentum_ids):
    momenta = momentum_ids.shape[0]
    wave_x = momentum_ids // LY
    wave_y = momentum_ids % LY
    sites = jnp.arange(momenta, dtype=jnp.int32)
    site_x = sites // LY
    site_y = sites % LY
    phase = (
        wave_x[:, None] * site_x[None, :] % LX * LY + wave_y[:, None] * site_y[None, :] % LY * LX
    )
    angle = 2.0 * jnp.pi / momenta * (phase % momenta).astype(jnp.float32)
    return (jnp.cos(angle), jnp.sin(angle), momenta)


def transforms(momentum_ids, groups):
    cos_table, sin_table, momenta = lattice_tables(momentum_ids)
    local_k = momenta // groups
    forward = jnp.stack(
        [jnp.stack([cos_table, sin_table], 1), jnp.stack([-sin_table, cos_table], 1)], 0
    )
    forward = (forward / momenta).astype(jnp.bfloat16)
    forward = forward.reshape(2, groups, local_k, 2, momenta).transpose(3, 4, 1, 0, 2)
    backward = jnp.stack(
        [jnp.stack([cos_table.T, -sin_table.T], 1), jnp.stack([sin_table.T, cos_table.T], 1)], 0
    ).astype(jnp.bfloat16)
    backward = backward.reshape(2, momenta, 2, groups, local_k).transpose(3, 2, 4, 0, 1)
    return (
        forward.reshape(2 * momenta, 2 * momenta),
        backward.reshape(2 * momenta, 2 * momenta),
    )


def drive(window_start, row_times):
    phase = ((window_start[0] + row_times) % DRIVE).astype(jnp.float32)
    return U_BASE * (1.0 + 0.5 * jnp.sin(2.0 * jnp.pi / DRIVE * phase))


def born_kernel(pieces, *refs):
    x_refs = refs[:pieces]
    forward_ref, backward_ref, weight_ref, mask_ref, out_ref = refs[pieces:]
    half = forward_ref.shape[0] // 2
    table = forward_ref[...]
    weight = -weight_ref[0]
    less = jnp.dot(
        table,
        jnp.concatenate([ref[0, 0] for ref in x_refs], axis=0),
        preferred_element_type=jnp.float32,
    )
    more = jnp.dot(
        table,
        jnp.concatenate([ref[0, 1] for ref in x_refs], axis=0),
        preferred_element_type=jnp.float32,
    )
    less_re, less_im = (less[:half], less[half:])
    more_re, more_im = (more[:half], more[half:])
    square_re = less_re * less_re - less_im * less_im
    square_im = 2.0 * less_re * less_im
    sigma_less = jnp.concatenate(
        [
            (weight * (square_re * more_re + square_im * more_im)).astype(jnp.bfloat16),
            (weight * (square_im * more_re - square_re * more_im)).astype(jnp.bfloat16),
        ],
        axis=0,
    )
    other_re = more_re * more_re - more_im * more_im
    other_im = 2.0 * more_re * more_im
    sigma_more = jnp.concatenate(
        [
            (weight * (other_re * less_re + other_im * less_im)).astype(jnp.bfloat16),
            (weight * (other_im * less_re - other_re * less_im)).astype(jnp.bfloat16),
        ],
        axis=0,
    )
    back = backward_ref[...]
    less_mom = jnp.dot(back, sigma_less, preferred_element_type=jnp.float32)
    more_mom = jnp.dot(back, sigma_more, preferred_element_type=jnp.float32)
    ret = (mask_ref[0] * (more_mom - less_mom)).astype(jnp.bfloat16)
    _, _, _, depth, width = out_ref.shape
    out_ref[:, 0, 0] = less_mom.astype(jnp.bfloat16).reshape(pieces, depth, width)
    out_ref[:, 1, 0] = ret.reshape(pieces, depth, width)


def born(spread, forward, backward, weight, mask):
    pieces = len(spread)
    sub_rows, _, depth, width = spread[0].shape
    size = pieces * depth
    out_shape = (pieces, 2, sub_rows, depth, width)
    return pl.pallas_call(
        functools.partial(born_kernel, pieces),
        grid=(sub_rows,),
        in_specs=[pl.BlockSpec((1, 2, depth, width), lambda i: (i, 0, 0, 0))] * pieces
        + [
            pl.BlockSpec((size, size), lambda i: (0, 0)),
            pl.BlockSpec((size, size), lambda i: (0, 0)),
            pl.BlockSpec((1, 1, width), lambda i: (i, 0, 0)),
            pl.BlockSpec((1, 1, width), lambda i: (i, 0, 0)),
        ],
        out_specs=pl.BlockSpec((pieces, 2, 1, depth, width), lambda i: (0, 0, i, 0, 0)),
        out_shape=jax.ShapeDtypeStruct(out_shape, jnp.bfloat16),
        compiler_params=pltpu.CompilerParams(vmem_limit_bytes=VMEM_BYTES),
        cost_estimate=pl.CostEstimate(
            flops=8 * size * size * sub_rows * width,
            bytes_accessed=8 * size * sub_rows * width,
            transcendentals=0,
        ),
        name="born",
    )(*spread, forward, backward, weight, mask)


def sigma_rows(ref, part, index):
    pieces, _, _, sub_rows, width = ref.shape
    return ref[:, part, index].reshape(pieces * sub_rows, width)


def collide_kernel(plan, order_ref, *refs):
    n_ret, n_less, first_step, first_col, done_cols, has_total, has_lesser, has_rest = plan
    refs = list(refs)
    ret_refs = [refs.pop(0) for _ in range(n_ret)]
    less_refs = [refs.pop(0) for _ in range(n_less)]
    lesser_ref = refs.pop(0) if has_lesser else None
    gap_less_ref, gap_more_ref = (refs.pop(0), refs.pop(0))
    total_ref = refs.pop(0) if has_total else None
    if has_total:
        refs.pop(0)
    out_ref = refs.pop(0)
    rest_ref = refs.pop(0) if has_rest else None
    block, steps, cols = gap_less_ref.shape[1:]
    pieces, _, _, sub_rows, _ = less_refs[0].shape
    rows = pieces * sub_rows
    step_index = first_step + lax.broadcasted_iota(jnp.int32, (steps, cols), 0)
    upper = step_index <= first_col + lax.broadcasted_iota(jnp.int32, (steps, cols), 1)
    for index in range(block):

        def advanced(part):
            gap = gap_less_ref[part, index].astype(jnp.float32)
            gap = gap - gap_more_ref[part, index].astype(jnp.float32)
            return jnp.where(upper, gap, 0.0).astype(jnp.bfloat16)

        re = [sigma_rows(ref, 0, index) for ref in less_refs]
        im = [sigma_rows(ref, 1, index) for ref in less_refs]
        top, low = (re + [-v for v in im], im + re)
        right = [advanced(0), advanced(1)]
        if has_lesser:
            re = [sigma_rows(ref, 0, index) for ref in ret_refs]
            im = [sigma_rows(ref, 1, index) for ref in ret_refs]
            top, low = (top + re + [-v for v in im], low + im + re)
            right = right + [lesser_ref[0, index], lesser_ref[1, index]]
        left = jnp.concatenate(
            [jnp.concatenate(top, axis=1), jnp.concatenate(low, axis=1)], axis=0
        )
        product = jnp.dot(
            left, jnp.concatenate(right, axis=0), preferred_element_type=jnp.float32
        )
        for part in range(2):
            value = product[part * rows : (part + 1) * rows]
            if has_total:
                value = total_ref[part, index] + value
            done = (TIME_STEP * value[:, :done_cols]).astype(out_ref.dtype)
            for piece in range(pieces):
                first = pl.multiple_of(order_ref[piece] * sub_rows, sub_rows)
                out_ref[part, index, pl.ds(first, sub_rows), :] = done[
                    piece * sub_rows : (piece + 1) * sub_rows
                ]
            if has_rest:
                rest_ref[part, index] = value[:, done_cols:]


def collide(order, rets, lesses, less_all, more_all, carried, first_step, first_col, done_cols):
    pieces, _, local_k, sub_rows, _ = lesses[0].shape
    col_count = less_all.shape[3]
    rows, steps, cols = (pieces * sub_rows, sum(s.shape[4] for s in lesses), col_count - first_col)
    block = min(MOMENTA_BLOCK, local_k)
    has_rest = done_cols < cols

    def sigma_spec(array):
        shape = (pieces, 2, block, sub_rows, array.shape[4])
        return pl.BlockSpec(shape, lambda k, order: (0, 0, k, 0, 0))

    arrays, specs = ([*rets, *lesses], [sigma_spec(a) for a in (*rets, *lesses)])
    if rets:
        arrays.append(less_all)
        specs.append(
            pl.BlockSpec((2, block, col_count, cols), lambda k, order: (0, k, 0, first_col // cols))
        )
    gap_index = (first_step // steps, first_col // cols)
    gap_spec = pl.BlockSpec((2, block, steps, cols), lambda k, order: (0, k, *gap_index))
    arrays += [less_all, more_all]
    specs += [gap_spec, gap_spec]
    aliases = {}
    if carried is not None:
        arrays += list(carried)
        specs += [
            pl.BlockSpec((2, block, rows, cols), lambda k, order: (0, k, 0, 0)),
            pl.BlockSpec(memory_space=pl.ANY),
        ]
        aliases = {len(arrays): 0}
    out_specs = [
        pl.BlockSpec((2, block, rows, done_cols), lambda k, order: (0, k, 0, first_col // done_cols))
    ]
    out_shape = [jax.ShapeDtypeStruct((2, local_k, rows, col_count), jnp.bfloat16)]
    if has_rest:
        rest = cols - done_cols
        out_specs.append(pl.BlockSpec((2, block, rows, rest), lambda k, order: (0, k, 0, 0)))
        out_shape.append(jax.ShapeDtypeStruct((2, local_k, rows, rest), jnp.float32))
    plan = (
        len(rets),
        len(lesses),
        first_step,
        first_col,
        done_cols,
        carried is not None,
        bool(rets),
        has_rest,
    )
    depth = steps + (col_count if rets else 0)
    results = pl.pallas_call(
        functools.partial(collide_kernel, plan),
        grid_spec=pltpu.PrefetchScalarGridSpec(
            num_scalar_prefetch=1, grid=(local_k // block,), in_specs=specs, out_specs=out_specs
        ),
        out_shape=out_shape,
        input_output_aliases=aliases,
        compiler_params=pltpu.CompilerParams(vmem_limit_bytes=VMEM_BYTES),
        cost_estimate=pl.CostEstimate(
            flops=8 * local_k * rows * depth * cols,
            bytes_accessed=4 * local_k * (depth + steps) * (cols + rows)
            + 12 * local_k * rows * cols,
            transcendentals=0,
        ),
        name="collide",
    )(order, *arrays)
    return (results[1] if has_rest else None, results[0])


def on_device(lesser, greater, momentum_ids, window_start):
    _, local_k, row_count, col_count = lesser.shape
    groups, ranks = (lax.axis_size("mom"), lax.axis_size("trow"))
    group = lax.axis_index("mom")
    sub_rows = row_count // groups
    order = group ^ jnp.arange(groups, dtype=jnp.int32)
    far, near = (list(range(groups // 2, groups)), list(range(1, groups // 2)))
    offsets = [d for pair in zip(far, near + [0]) for d in pair if d]

    def send(array, offset, first_rank=0):
        pairs = [
            (g * ranks + r, (g ^ offset) * ranks + r)
            for g in range(groups)
            for r in range(first_rank, ranks)
        ]
        return lax.ppermute(array, ("mom", "trow"), pairs)

    row_first = lax.axis_index("trow") * row_count + group * sub_rows
    row_times = row_first + jnp.arange(sub_rows, dtype=jnp.int32)
    width = col_count // 4

    def pack(offset, first, count):
        def rows_of(array):
            return lax.dynamic_slice(
                array,
                (0, 0, (group ^ offset) * sub_rows, first),
                (2, local_k, sub_rows, count),
            )

        both = jnp.stack([rows_of(lesser), rows_of(greater)])
        both = both.transpose(3, 0, 1, 2, 4)
        return both.reshape(sub_rows, 2, 2 * local_k, count)

    halves = [(0, 2 * width), (2 * width, 2 * width)]
    spreads = []
    for first, count in halves:
        spread = {0: pack(0, first, count)}
        for d in offsets:
            spread[d] = send(pack(d, first, count), d)
        spreads.append([spread[d] for d in range(groups)])

    less_all = lax.all_gather(lesser, "trow", axis=2, tiled=True)
    more_all = lax.all_gather(greater, "trow", axis=2, tiled=True)
    forward, backward = transforms(
        momentum_ids.reshape(groups, local_k)[order].reshape(-1), groups
    )
    row_drive = drive(window_start, row_times)

    def born_part(part):
        first, count = halves[part]
        col_index = first + jnp.arange(count, dtype=jnp.int32)
        weight = row_drive[:, None] * drive(window_start, col_index)[None, :]
        mask = (row_times[:, None] >= col_index[None, :]).astype(jnp.float32)
        return born(spreads[part], forward, backward, weight[:, None], mask[:, None])

    def exchange(sigma, kind, first, count, col_first):
        first_rank = 0 if kind == 0 else min(r for r in range(ranks) if (r + 1) * row_count > col_first)
        got = {}
        for d in [*offsets, 0]:
            piece = sigma[d, kind, :, :, first : first + count].transpose(1, 0, 2)
            got[d] = send(piece, d, first_rank) if d else piece
        pieces = jnp.stack([got[d] for d in range(groups)])
        pieces = pieces.reshape(groups, 2, local_k, sub_rows, count)
        if sub_rows % 16 == 0:
            return pieces
        pieces = pieces[order].transpose(1, 2, 0, 3, 4)
        return pieces.reshape(1, 2, local_k, groups * sub_rows, count)

    sigma = born_part(0)
    ret_low = exchange(sigma, 1, 0, 2 * width, 0)
    less_low = exchange(sigma, 0, 0, 2 * width, 0)
    sigma = born_part(1)
    ret_mid = exchange(sigma, 1, 0, width, 2 * width)
    ret_high = exchange(sigma, 1, width, width, 3 * width)
    less_mid = exchange(sigma, 0, 0, width, 2 * width)
    less_high = exchange(sigma, 0, width, width, 3 * width)
    if sub_rows % 16:
        order = jnp.zeros((1,), jnp.int32)
    carried = collide(
        order, [ret_low, ret_mid, ret_high], [less_low], less_all, more_all, None, 0, 0, 2 * width
    )
    carried = collide(
        order, [], [less_mid], less_all, more_all, carried, 2 * width, 2 * width, width
    )
    carried = collide(
        order, [], [less_high], less_all, more_all, carried, 3 * width, 3 * width, width
    )
    return carried[1]


def solution(mesh):
    return jax.shard_map(
        on_device,
        mesh=mesh,
        in_specs=(P(None, "mom", "trow", None), P(None, "mom", "trow", None), P(), P()),
        out_specs=P(None, "mom", "trow", None),
        check_vma=False,
    )
```

time: 881 us -> 880 us (level)
  waiting for transfers between devices: 657 us -> 347 us
  starting transfers between devices: 20.8 us -> 315 us
  local copies, waits for them, and re-layouts: 55.1 us -> 75.9 us
    all_to_all x4 -> x0, waiting for transfers between devices: 655 us -> none  [swap_groups(): return lax.all_to_all(part, 'mom', split_axis=0, concat_axis=0, tiled=True)]
    ppermute x0 -> x56, waiting for transfers between devices: none -> 346 us  [send(): return lax.ppermute(array, ('mom', 'trow'), pairs)]
    ppermute x0 -> x56, starting transfers between devices: none -> 315 us  [send(): return lax.ppermute(array, ('mom', 'trow'), pairs)]
    transpose x0 -> x25, local copies, waits for them, and re-layouts: none -> 34.2 us  [the longest x16 20.7 us: pack(): both = both.transpose(3, 0, 1, 2, 4)]
    reshape x2 -> x1, local copies, waits for them, and re-layouts: 26.8 us -> 0.08 us  [on_device(): momentum_ids.reshape(groups, local_k)[order].reshape(-1)]
    all_to_all x2 -> x0, local copies, waits for them, and re-layouts: 25 us -> none  [swap_groups(): return lax.all_to_all(part, 'mom', split_axis=0, concat_axis=0, tiled=True)]
    all_to_all x4 -> x0, starting transfers between devices: 20.8 us -> none  [swap_groups(): return lax.all_to_all(part, 'mom', split_axis=0, concat_axis=0, tiled=True)]
    another operation x0 -> x8, local copies, waits for them, and re-layouts: none -> 14.4 us  [the longest x2 13.4 us: pack(): both = jnp.stack([rows_of(lesser), rows_of(greater)])]
  transfers between devices with their start and end apart: 6 -> 58, of which waited for: 4 -> 19; matrix products, arithmetic and copies ran while one was open for 8% -> 10% of each run, Pallas kernels for 5% -> 5%
where the time goes in v2:
time: 880 us; the launch traced here: 872 us
  waiting for transfers between devices  347 us (39%)
  starting transfers between devices  315 us (36%)
  Pallas kernels  106 us (12%)
  local copies, waits for them, and re-layouts  75.9 us (9%)
  between operations  16 us (2%)
  other arithmetic  12.4 us (1%)
    ppermute x56, waiting for transfers between devices, send(): return lax.ppermute(array, ('mom', 'trow'), pairs)  346 us
    ppermute x56, starting transfers between devices, send(): return lax.ppermute(array, ('mom', 'trow'), pairs)  315 us
    pallas_call x3, Pallas kernels, collide(): pl.pallas_call(functools.partial(collide_kernel, plan), grid_spec=pltpu.P...  64.8 us
    pallas_call x2, Pallas kernels, born(): pl.pallas_call(functools.partial(born_kernel, pieces), grid=(sub_rows,),...  40.8 us
    transpose x16, local copies, waits for them, and re-layouts, pack(): both = both.transpose(3, 0, 1, 2, 4)  20.7 us
  transfers between devices with their start and end apart: 58, of which 19 were waited for; matrix products, arithmetic and copies ran while one was open for 10% of the time, Pallas kernels for 5%

profile of v2, /device:TPU:7, one launch (start us, length us, event | category | flops | bytes accessed | tf_op | source)
XLA Modules:
  0.0 872.0 jit_solution(5391410348840914982)
XLA Ops:
  8.1 5.7 dynamic-slice_bitcast_fusion.1
  13.7 7.7 dynamic-slice_bitcast_fusion
  51.5 25.2 %collective-permute-done.refs_1_ = bf16[16,2,64,256]{3,2,1,0:T(8,128)(2,1)} collective-permute-done((bf16[16,2,64,256]{3,2,1,0:T(8,128)(2,1)}, bf16[16,2,64,256]{3,2,1,0:T(8,128)(2,1)}, u32[]{:S(2)}, u32[]{:S(2)}) %collective-permute-start) | collective-permute-done | bytes 1048608 | tf_op jit(solution)/shard_map/ppermute | solution.py:271
  76.7 17.7 %collective-permute-start.6 = (bf16[16,2,64,256]{3,2,1,0:T(8,128)(2,1)}, bf16[16,2,64,256]{3,2,1,0:T(8,128)(2,1)}, u32[]{:S(2)}, u32[]{:S(2)}) collective-permute-start(bf16[16,2,64,256]{3,2,1,0:T(8,128)(2,1)} %bitcast.31), channel_id=1, source_target_pairs={{0,28},{1,29},{2,30},{3,31},{4,24},{5,25},{6,26},{7,27},{8,20},{9,... | collective-permute-start | bytes 3145736 | tf_op jit(solution)/shard_map/ppermute | solution.py:271
  95.6 18.2 %collective-permute-done.1.refs_2_ = bf16[16,2,64,256]{3,2,1,0:T(8,128)(2,1)} collective-permute-done((bf16[16,2,64,256]{3,2,1,0:T(8,128)(2,1)}, bf16[16,2,64,256]{3,2,1,0:T(8,128)(2,1)}, u32[]{:S(2)}, u32[]{:S(2)}) %collective-permute-start.1) | collective-permute-done | bytes 1048608 | tf_op jit(solution)/shard_map/ppermute | solution.py:271
  132.7 33.3 %collective-permute-done.3.refs_4_ = bf16[16,2,64,256]{3,2,1,0:T(8,128)(2,1)} collective-permute-done((bf16[16,2,64,256]{3,2,1,0:T(8,128)(2,1)}, bf16[16,2,64,256]{3,2,1,0:T(8,128)(2,1)}, u32[]{:S(2)}, u32[]{:S(2)}) %collective-permute-start.3) | collective-permute-done | bytes 1048608 | tf_op jit(solution)/shard_map/ppermute | solution.py:271
  167.3 42.4 %collective-permute-start.25 = (bf16[16,2,64,256]{3,2,1,0:T(8,128)(2,1)}, bf16[16,2,64,256]{3,2,1,0:T(8,128)(2,1)}, u32[]{:S(2)}, u32[]{:S(2)}) collective-permute-start(bf16[16,2,64,256]{3,2,1,0:T(8,128)(2,1)} %bitcast.107), channel_id=1, source_target_pairs={{0,20},{1,21},{2,22},{3,23},{4,16},{5,17},{6,18},{7,19},{8,28},{9,... | collective-permute-start | bytes 3145736 | tf_op jit(solution)/shard_map/ppermute | solution.py:271
  209.8 44.0 %collective-permute-start.24 = (bf16[16,2,64,256]{3,2,1,0:T(8,128)(2,1)}, bf16[16,2,64,256]{3,2,1,0:T(8,128)(2,1)}, u32[]{:S(2)}, u32[]{:S(2)}) collective-permute-start(bf16[16,2,64,256]{3,2,1,0:T(8,128)(2,1)} %bitcast.103), channel_id=1, source_target_pairs={{0,16},{1,17},{2,18},{3,19},{4,20},{5,21},{6,22},{7,23},{8,24},{9,... | collective-permute-start | bytes 3145736 | tf_op jit(solution)/shard_map/ppermute | solution.py:271
  257.0 20.3 %born.2 = bf16[8,2,16,64,256]{4,3,2,1,0:T(8,128)(2,1)} custom-call(bf16[16,2,64,256]{3,2,1,0:T(8,128)(2,1)} %bitcast.391, bf16[16,2,64,256]{3,2,1,0:T(8,128)(2,1)} %collective-permute-done.refs_1_, bf16[16,2,64,256]{3,2,1,0:T(8,128)(2,1)} %collective-permute-done.1.refs_2_, bf16[16,2,64,256]{3,2,1,0:T(8,128)(2,1)} %collective-permute-done.2.refs_3_, ...), custom_call_target="tpu_custom_call" | custom-call | flops 8589934592 | bytes 16777216 | tf_op jit(solution)/shard_map/born/pallas_call | solution.py:109
  286.2 61.5 %collective-permute-done.25.refs_5_ = bf16[16,2,64,256]{3,2,1,0:T(8,128)(2,1)} collective-permute-done((bf16[16,2,64,256]{3,2,1,0:T(8,128)(2,1)}, bf16[16,2,64,256]{3,2,1,0:T(8,128)(2,1)}, u32[]{:S(2)}, u32[]{:S(2)}) %collective-permute-start.25) | collective-permute-done | bytes 1048608 | tf_op jit(solution)/shard_map/ppermute | solution.py:271
  350.8 19.4 %collective-permute-done.24.refs_4_ = bf16[16,2,64,256]{3,2,1,0:T(8,128)(2,1)} collective-permute-done((bf16[16,2,64,256]{3,2,1,0:T(8,128)(2,1)}, bf16[16,2,64,256]{3,2,1,0:T(8,128)(2,1)}, u32[]{:S(2)}, u32[]{:S(2)}) %collective-permute-start.24) | collective-permute-done | bytes 1048608 | tf_op jit(solution)/shard_map/ppermute | solution.py:271
  370.2 20.5 %born.3 = bf16[8,2,16,64,256]{4,3,2,1,0:T(8,128)(2,1)} custom-call(bf16[16,2,64,256]{3,2,1,0:T(8,128)(2,1)} %bitcast.389, bf16[16,2,64,256]{3,2,1,0:T(8,128)(2,1)} %collective-permute-done.21.refs_1_, bf16[16,2,64,256]{3,2,1,0:T(8,128)(2,1)} %copy-done.45, bf16[16,2,64,256]{3,2,1,0:T(8,128)(2,1)} %collective-permute-done.23.refs_3_, ...), custom_call_target="tpu_custom_call" | custom-call | flops 8589934592 | bytes 16777216 | tf_op jit(solution)/shard_map/born/pallas_call | solution.py:109
  395.3 45.2 %collective-permute-start.16 = (bf16[64,16,128]{2,0,1:T(8,128)(2,1)}, bf16[64,16,128]{2,0,1:T(8,128)(2,1)S(1)}, u32[]{:S(2)}, u32[]{:S(2)}) collective-permute-start(bf16[64,16,128]{2,0,1:T(8,128)(2,1)} %get-tuple-element.81), channel_id=1, source_target_pairs={{0,12},{1,13},{2,14},{3,15},{4,8},{5,9},{6,10},{7,11},{8,4},{9,5},... | collective-permute-start | bytes 786440 | tf_op jit(solution)/shard_map/ppermute | solution.py:271
  451.6 7.2 collective-permute-done.36
  481.6 17.9 %collective-permute-start.44 = (bf16[64,16,128]{2,0,1:T(8,128)(2,1)S(1)}, bf16[64,16,128]{2,0,1:T(8,128)(2,1)S(1)}, u32[]{:S(2)}, u32[]{:S(2)}) collective-permute-start(bf16[64,16,128]{2,0,1:T(8,128)(2,1)S(1)} %copy-done.28), channel_id=1, source_target_pairs={{3,15},{7,11},{11,7},{15,3},{19,31},{23,27},{27,23},{31,19}} | collective-permute-start | bytes 786440 | tf_op jit(solution)/shard_map/ppermute | solution.py:271
  499.5 7.1 collective-permute-start.43
  509.3 9.0 %collective-permute-start.11 = (bf16[64,16,128]{2,0,1:T(8,128)(2,1)S(1)}, bf16[64,16,128]{2,0,1:T(8,128)(2,1)S(1)}, u32[]{:S(2)}, u32[]{:S(2)}) collective-permute-start(bf16[64,16,128]{2,0,1:T(8,128)(2,1)S(1)} %copy-done.39), channel_id=1, source_target_pairs={{0,20},{1,21},{2,22},{3,23},{4,16},{5,17},{6,18},{7,19},{8,28},{9,... | collective-permute-start | bytes 786440 | tf_op jit(solution)/shard_map/ppermute | solution.py:271
  518.3 7.5 collective-permute-start.10
  531.1 10.2 %collective-permute-done.45 = bf16[64,16,128]{2,0,1:T(8,128)(2,1)S(1)} collective-permute-done((bf16[64,16,128]{2,0,1:T(8,128)(2,1)S(1)}, bf16[64,16,128]{2,0,1:T(8,128)(2,1)S(1)}, u32[]{:S(2)}, u32[]{:S(2)}) %collective-permute-start.45) | collective-permute-done | bytes 262176 | tf_op jit(solution)/shard_map/ppermute | solution.py:271
  544.2 8.4 collective-permute-done.11
  570.2 23.7 %collective-permute-done.8 = bf16[64,16,128]{2,0,1:T(8,128)(2,1)S(1)} collective-permute-done((bf16[64,16,128]{2,0,1:T(8,128)(2,1)S(1)}, bf16[64,16,128]{2,0,1:T(8,128)(2,1)S(1)}, u32[]{:S(2)}, u32[]{:S(2)}) %collective-permute-start.8) | collective-permute-done | bytes 262176 | tf_op jit(solution)/shard_map/ppermute | solution.py:271
  598.9 40.0 %collective-permute-start.18 = (bf16[64,16,128]{2,0,1:T(8,128)(2,1)S(1)}, bf16[64,16,128]{2,0,1:T(8,128)(2,1)S(1)}, u32[]{:S(2)}, u32[]{:S(2)}) collective-permute-start(bf16[64,16,128]{2,0,1:T(8,128)(2,1)S(1)} %get-tuple-element.47), channel_id=1, source_target_pairs={{0,20},{1,21},{2,22},{3,23},{4,16},{5,17},{6,18},{7,19},{8,28},{9,... | collective-permute-start | bytes 786440 | tf_op jit(solution)/shard_map/ppermute | solution.py:271
  639.6 50.1 %collective-permute-done.18 = bf16[64,16,128]{2,0,1:T(8,128)(2,1)S(1)} collective-permute-done((bf16[64,16,128]{2,0,1:T(8,128)(2,1)S(1)}, bf16[64,16,128]{2,0,1:T(8,128)(2,1)S(1)}, u32[]{:S(2)}, u32[]{:S(2)}) %collective-permute-start.18) | collective-permute-done | bytes 262176 | tf_op jit(solution)/shard_map/ppermute | solution.py:271
  697.3 9.9 %collective-permute-done.51 = bf16[64,16,256]{2,0,1:T(8,128)(2,1)S(1)} collective-permute-done((bf16[64,16,256]{2,0,1:T(8,128)(2,1)S(1)}, bf16[64,16,256]{2,0,1:T(8,128)(2,1)S(1)}, u32[]{:S(2)}, u32[]{:S(2)}) %collective-permute-start.51) | collective-permute-done | bytes 524320 | tf_op jit(solution)/shard_map/ppermute | solution.py:271
  712.3 6.1 collective-permute-done.50
  725.9 5.5 collective-permute-done.34
  731.4 12.6 %collective-permute-done.33 = bf16[64,16,256]{2,0,1:T(8,128)(2,1)S(1)} collective-permute-done((bf16[64,16,256]{2,0,1:T(8,128)(2,1)S(1)}, bf16[64,16,256]{2,0,1:T(8,128)(2,1)S(1)}, u32[]{:S(2)}, u32[]{:S(2)}) %collective-permute-start.33) | collective-permute-done | bytes 524320 | tf_op jit(solution)/shard_map/ppermute | solution.py:271
  748.7 32.8 %collective-permute-done.32 = bf16[64,16,256]{2,0,1:T(8,128)(2,1)S(1)} collective-permute-done((bf16[64,16,256]{2,0,1:T(8,128)(2,1)S(1)}, bf16[64,16,256]{2,0,1:T(8,128)(2,1)S(1)}, u32[]{:S(2)}, u32[]{:S(2)}) %collective-permute-start.32) | collective-permute-done | bytes 524320 | tf_op jit(solution)/shard_map/ppermute | solution.py:271
  781.8 10.1 %collective-permute-done.31 = bf16[64,16,256]{2,0,1:T(8,128)(2,1)S(1)} collective-permute-done((bf16[64,16,256]{2,0,1:T(8,128)(2,1)S(1)}, bf16[64,16,256]{2,0,1:T(8,128)(2,1)S(1)}, u32[]{:S(2)}, u32[]{:S(2)}) %collective-permute-start.31) | collective-permute-done | bytes 524320 | tf_op jit(solution)/shard_map/ppermute | solution.py:271
  800.0 35.5 %collide.3 = (bf16[2,32,128,512]{3,2,1,0:T(8,128)(2,1)}, f32[2,32,128,256]{3,2,1,0:T(8,128)}) custom-call(s32[8]{0:T(128)} %iota_xor_fusion.order_ref, bf16[8,2,32,16,256]{4,3,2,1,0:T(8,128)(2,1)} %copy-done, bf16[8,2,32,16,128]{4,3,2,1,0:T(8,128)(2,1)} %copy-done.7, bf16[8,2,32,16,128]{4,3,2,1,0:T(8,128)(2,1)} %copy-done.6, ...), custom_call_target="tpu_custom_call" | custom-call | flops 12884901888 | bytes 109051904 | tf_op jit(solution)/shard_map/collide/pallas_call | solution.py:237
  835.4 15.9 %collide.4 = (bf16[2,32,128,512]{3,2,1,0:T(8,128)(2,1)}, f32[2,32,128,128]{3,2,1,0:T(8,128)}) custom-call(s32[8]{0:T(128)} %iota_xor_fusion.order_ref, bf16[8,2,32,16,128]{4,3,2,1,0:T(8,128)(2,1)} %copy-done.4, bf16[2,32,512,512]{3,2,1,0:T(8,128)(2,1)} %all-gather.3.cloned.1.call-done.refs_4_.refs_5_.refs_1_, ...), custom_call_target="tpu_custom_call", output_to_operand_aliasing={{0}: (5, {})} | custom-call | flops 1073741824 | bytes 25165824 | tf_op jit(solution)/shard_map/collide/pallas_call | solution.py:237
  851.3 13.4 %collide.5 = bf16[2,32,128,512]{3,2,1,0:T(8,128)(2,1)} custom-call(s32[8]{0:T(128)} %iota_xor_fusion.order_ref, bf16[8,2,32,16,128]{4,3,2,1,0:T(8,128)(2,1)} %copy-done.5, bf16[2,32,512,512]{3,2,1,0:T(8,128)(2,1)} %all-gather.3.cloned.1.call-done.refs_4_.refs_5_.refs_1_, ...), custom_call_target="tpu_custom_call", output_to_operand_aliasing={{}: (5, {})} | custom-call | flops 536870912 | bytes 14680064 | tf_op jit(solution)/shard_map/collide/pallas_call | solution.py:237
  (330 shorter events, 172.0 us)
Async XLA Ops:
  6.5 793.4 %all-gather.3.cloned.1.call-start = ((), (), s32[]{:S(2)}) async-start(), calls=%async_computation | async-start | bytes 41943040 | tf_op jit(solution)/shard_map/all_gather | solution.py:297
  7.3 792.7 %all-gather.5.cloned.1.call-start = ((), (), s32[]{:S(2)}) async-start(), calls=%async_computation.1 | async-start | bytes 41943040 | tf_op jit(solution)/shard_map/all_gather | solution.py:298
  22.9 53.8 %collective-permute-start = (bf16[16,2,64,256]{3,2,1,0:T(8,128)(2,1)}, bf16[16,2,64,256]{3,2,1,0:T(8,128)(2,1)}, u32[]{:S(2)}, u32[]{:S(2)}) collective-permute-start(bf16[16,2,64,256]{3,2,1,0:T(8,128)(2,1)} %bitcast.7), channel_id=1, source_target_pairs={{0,4},{1,5},{2,6},{3,7},{4,0},{5,1},{6,2},{7,3},{8,12},{9,13},{10,... | collective-permute-start | bytes 3145736 | tf_op jit(solution)/shard_map/ppermute | solution.py:271
  24.7 69.7 %collective-permute-start.2 = (bf16[16,2,64,256]{3,2,1,0:T(8,128)(2,1)}, bf16[16,2,64,256]{3,2,1,0:T(8,128)(2,1)}, u32[]{:S(2)}, u32[]{:S(2)}) collective-permute-start(bf16[16,2,64,256]{3,2,1,0:T(8,128)(2,1)} %bitcast.15), channel_id=1, source_target_pairs={{0,12},{1,13},{2,14},{3,15},{4,8},{5,9},{6,10},{7,11},{8,4},{9,5},... | collective-permute-start | bytes 3145736 | tf_op jit(solution)/shard_map/ppermute | solution.py:271
  28.4 85.4 %collective-permute-start.1 = (bf16[16,2,64,256]{3,2,1,0:T(8,128)(2,1)}, bf16[16,2,64,256]{3,2,1,0:T(8,128)(2,1)}, u32[]{:S(2)}, u32[]{:S(2)}) collective-permute-start(bf16[16,2,64,256]{3,2,1,0:T(8,128)(2,1)} %bitcast.11), channel_id=1, source_target_pairs={{0,8},{1,9},{2,10},{3,11},{4,12},{5,13},{6,14},{7,15},{8,0},{9,1},... | collective-permute-start | bytes 3145736 | tf_op jit(solution)/shard_map/ppermute | solution.py:271
  30.0 83.8 %collective-permute-start.4 = (bf16[16,2,64,256]{3,2,1,0:T(8,128)(2,1)}, bf16[16,2,64,256]{3,2,1,0:T(8,128)(2,1)}, u32[]{:S(2)}, u32[]{:S(2)}) collective-permute-start(bf16[16,2,64,256]{3,2,1,0:T(8,128)(2,1)} %bitcast.23), channel_id=1, source_target_pairs={{0,20},{1,21},{2,22},{3,23},{4,16},{5,17},{6,18},{7,19},{8,28},{9,... | collective-permute-start | bytes 3145736 | tf_op jit(solution)/shard_map/ppermute | solution.py:271
  33.8 132.2 %collective-permute-start.3 = (bf16[16,2,64,256]{3,2,1,0:T(8,128)(2,1)}, bf16[16,2,64,256]{3,2,1,0:T(8,128)(2,1)}, u32[]{:S(2)}, u32[]{:S(2)}) collective-permute-start(bf16[16,2,64,256]{3,2,1,0:T(8,128)(2,1)} %bitcast.19), channel_id=1, source_target_pairs={{0,16},{1,17},{2,18},{3,19},{4,20},{5,21},{6,22},{7,23},{8,24},{9,... | collective-permute-start | bytes 3145736 | tf_op jit(solution)/shard_map/ppermute | solution.py:271
  76.7 90.6 %collective-permute-start.6 = (bf16[16,2,64,256]{3,2,1,0:T(8,128)(2,1)}, bf16[16,2,64,256]{3,2,1,0:T(8,128)(2,1)}, u32[]{:S(2)}, u32[]{:S(2)}) collective-permute-start(bf16[16,2,64,256]{3,2,1,0:T(8,128)(2,1)} %bitcast.31), channel_id=1, source_target_pairs={{0,28},{1,29},{2,30},{3,31},{4,24},{5,25},{6,26},{7,27},{8,20},{9,... | collective-permute-start | bytes 3145736 | tf_op jit(solution)/shard_map/ppermute | solution.py:271
  94.4 115.3 %collective-permute-start.5 = (bf16[16,2,64,256]{3,2,1,0:T(8,128)(2,1)}, bf16[16,2,64,256]{3,2,1,0:T(8,128)(2,1)}, u32[]{:S(2)}, u32[]{:S(2)}) collective-permute-start(bf16[16,2,64,256]{3,2,1,0:T(8,128)(2,1)} %bitcast.27), channel_id=1, source_target_pairs={{0,24},{1,25},{2,26},{3,27},{4,28},{5,29},{6,30},{7,31},{8,16},{9,... | collective-permute-start | bytes 3145736 | tf_op jit(solution)/shard_map/ppermute | solution.py:271
  113.8 140.0 %collective-permute-start.21 = (bf16[16,2,64,256]{3,2,1,0:T(8,128)(2,1)}, bf16[16,2,64,256]{3,2,1,0:T(8,128)(2,1)}, u32[]{:S(2)}, u32[]{:S(2)}) collective-permute-start(bf16[16,2,64,256]{3,2,1,0:T(8,128)(2,1)} %bitcast.91), channel_id=1, source_target_pairs={{0,4},{1,5},{2,6},{3,7},{4,0},{5,1},{6,2},{7,3},{8,12},{9,13},{10,... | collective-permute-start | bytes 3145736 | tf_op jit(solution)/shard_map/ppermute | solution.py:271
  113.8 140.8 %collective-permute-start.23 = (bf16[16,2,64,256]{3,2,1,0:T(8,128)(2,1)}, bf16[16,2,64,256]{3,2,1,0:T(8,128)(2,1)}, u32[]{:S(2)}, u32[]{:S(2)}) collective-permute-start(bf16[16,2,64,256]{3,2,1,0:T(8,128)(2,1)} %bitcast.99), channel_id=1, source_target_pairs={{0,12},{1,13},{2,14},{3,15},{4,8},{5,9},{6,10},{7,11},{8,4},{9,5},... | collective-permute-start | bytes 3145736 | tf_op jit(solution)/shard_map/ppermute | solution.py:271
  166.1 120.0 %collective-permute-start.22 = (bf16[16,2,64,256]{3,2,1,0:T(8,128)(2,1)}, bf16[16,2,64,256]{3,2,1,0:T(8,128)(2,1)S(1)}, u32[]{:S(2)}, u32[]{:S(2)}) collective-permute-start(bf16[16,2,64,256]{3,2,1,0:T(8,128)(2,1)} %bitcast.95), channel_id=1, source_target_pairs={{0,8},{1,9},{2,10},{3,11},{4,12},{5,13},{6,14},{7,15},{8,0},{9,1},... | collective-permute-start | bytes 3145736 | tf_op jit(solution)/shard_map/ppermute | solution.py:271
  167.3 180.4 %collective-permute-start.25 = (bf16[16,2,64,256]{3,2,1,0:T(8,128)(2,1)}, bf16[16,2,64,256]{3,2,1,0:T(8,128)(2,1)}, u32[]{:S(2)}, u32[]{:S(2)}) collective-permute-start(bf16[16,2,64,256]{3,2,1,0:T(8,128)(2,1)} %bitcast.107), channel_id=1, source_target_pairs={{0,20},{1,21},{2,22},{3,23},{4,16},{5,17},{6,18},{7,19},{8,28},{9,... | collective-permute-start | bytes 3145736 | tf_op jit(solution)/shard_map/ppermute | solution.py:271
  209.8 160.4 %collective-permute-start.24 = (bf16[16,2,64,256]{3,2,1,0:T(8,128)(2,1)}, bf16[16,2,64,256]{3,2,1,0:T(8,128)(2,1)}, u32[]{:S(2)}, u32[]{:S(2)}) collective-permute-start(bf16[16,2,64,256]{3,2,1,0:T(8,128)(2,1)} %bitcast.103), channel_id=1, source_target_pairs={{0,16},{1,17},{2,18},{3,19},{4,20},{5,21},{6,22},{7,23},{8,24},{9,... | collective-permute-start | bytes 3145736 | tf_op jit(solution)/shard_map/ppermute | solution.py:271
  253.8 116.4 %collective-permute-start.27 = (bf16[16,2,64,256]{3,2,1,0:T(8,128)(2,1)S(1)}, bf16[16,2,64,256]{3,2,1,0:T(8,128)(2,1)}, u32[]{:S(2)}, u32[]{:S(2)}) collective-permute-start(bf16[16,2,64,256]{3,2,1,0:T(8,128)(2,1)S(1)} %bitcast.390), channel_id=1, source_target_pairs={{0,28},{1,29},{2,30},{3,31},{4,24},{5,25},{6,26},{7,27},{8,20},{9,... | collective-permute-start | bytes 3145736 | tf_op jit(solution)/shard_map/ppermute | solution.py:271
  254.6 115.6 %collective-permute-start.26 = (bf16[16,2,64,256]{3,2,1,0:T(8,128)(2,1)S(1)}, bf16[16,2,64,256]{3,2,1,0:T(8,128)(2,1)}, u32[]{:S(2)}, u32[]{:S(2)}) collective-permute-start(bf16[16,2,64,256]{3,2,1,0:T(8,128)(2,1)S(1)} %bitcast.388), channel_id=1, source_target_pairs={{0,24},{1,25},{2,26},{3,27},{4,28},{5,29},{6,30},{7,31},{8,16},{9,... | collective-permute-start | bytes 3145736 | tf_op jit(solution)/shard_map/ppermute | solution.py:271
  286.1 176.1 %collective-permute-start.17 = (bf16[64,16,128]{2,0,1:T(8,128)(2,1)}, bf16[64,16,128]{2,0,1:T(8,128)(2,1)}, u32[]{:S(2)}, u32[]{:S(2)}) collective-permute-start(bf16[64,16,128]{2,0,1:T(8,128)(2,1)} %get-tuple-element.80), channel_id=1, source_target_pairs={{0,16},{1,17},{2,18},{3,19},{4,20},{5,21},{6,22},{7,23},{8,24},{9,... | collective-permute-start | bytes 786440 | tf_op jit(solution)/shard_map/ppermute | solution.py:271
  347.7 99.5 %collective-permute-start.35 = (bf16[64,16,128]{2,0,1:T(8,128)(2,1)S(1)}, bf16[64,16,128]{2,0,1:T(8,128)(2,1)S(1)}, u32[]{:S(2)}, u32[]{:S(2)}) collective-permute-start(bf16[64,16,128]{2,0,1:T(8,128)(2,1)S(1)} %get-tuple-element.43), channel_id=1, source_target_pairs={{2,6},{3,7},{6,2},{7,3},{10,14},{11,15},{14,10},{15,11},{18,22},{1... | collective-permute-start | bytes 786440 | tf_op jit(solution)/shard_map/ppermute | solution.py:271
  395.3 69.1 %collective-permute-start.16 = (bf16[64,16,128]{2,0,1:T(8,128)(2,1)}, bf16[64,16,128]{2,0,1:T(8,128)(2,1)S(1)}, u32[]{:S(2)}, u32[]{:S(2)}) collective-permute-start(bf16[64,16,128]{2,0,1:T(8,128)(2,1)} %get-tuple-element.81), channel_id=1, source_target_pairs={{0,12},{1,13},{2,14},{3,15},{4,8},{5,9},{6,10},{7,11},{8,4},{9,5},... | collective-permute-start | bytes 786440 | tf_op jit(solution)/shard_map/ppermute | solution.py:271
  481.6 44.2 %collective-permute-start.44 = (bf16[64,16,128]{2,0,1:T(8,128)(2,1)S(1)}, bf16[64,16,128]{2,0,1:T(8,128)(2,1)S(1)}, u32[]{:S(2)}, u32[]{:S(2)}) collective-permute-start(bf16[64,16,128]{2,0,1:T(8,128)(2,1)S(1)} %copy-done.28), channel_id=1, source_target_pairs={{3,15},{7,11},{11,7},{15,3},{19,31},{23,27},{27,23},{31,19}} | collective-permute-start | bytes 786440 | tf_op jit(solution)/shard_map/ppermute | solution.py:271
  509.3 43.3 %collective-permute-start.11 = (bf16[64,16,128]{2,0,1:T(8,128)(2,1)S(1)}, bf16[64,16,128]{2,0,1:T(8,128)(2,1)S(1)}, u32[]{:S(2)}, u32[]{:S(2)}) collective-permute-start(bf16[64,16,128]{2,0,1:T(8,128)(2,1)S(1)} %copy-done.39), channel_id=1, source_target_pairs={{0,20},{1,21},{2,22},{3,23},{4,16},{5,17},{6,18},{7,19},{8,28},{9,... | collective-permute-start | bytes 786440 | tf_op jit(solution)/shard_map/ppermute | solution.py:271
  567.9 121.8 %collective-permute-start.55 = (bf16[64,16,256]{2,0,1:T(8,128)(2,1)S(1)}, bf16[64,16,256]{2,0,1:T(8,128)(2,1)S(1)}, u32[]{:S(2)}, u32[]{:S(2)}) collective-permute-start(bf16[64,16,256]{2,0,1:T(8,128)(2,1)S(1)} %get-tuple-element.13), channel_id=1, source_target_pairs={{0,28},{1,29},{2,30},{3,31},{4,24},{5,25},{6,26},{7,27},{8,20},{9,... | collective-permute-start | bytes 1572872 | tf_op jit(solution)/shard_map/ppermute | solution.py:271
  593.9 97.7 %collective-permute-start.54 = (bf16[64,16,256]{2,0,1:T(8,128)(2,1)S(1)}, bf16[64,16,256]{2,0,1:T(8,128)(2,1)S(1)}, u32[]{:S(2)}, u32[]{:S(2)}) collective-permute-start(bf16[64,16,256]{2,0,1:T(8,128)(2,1)S(1)} %get-tuple-element.14), channel_id=1, source_target_pairs={{0,24},{1,25},{2,26},{3,27},{4,28},{5,29},{6,30},{7,31},{8,16},{9,... | collective-permute-start | bytes 1572872 | tf_op jit(solution)/shard_map/ppermute | solution.py:271
  596.1 96.2 %collective-permute-start.53 = (bf16[64,16,256]{2,0,1:T(8,128)(2,1)S(1)}, bf16[64,16,256]{2,0,1:T(8,128)(2,1)S(1)}, u32[]{:S(2)}, u32[]{:S(2)}) collective-permute-start(bf16[64,16,256]{2,0,1:T(8,128)(2,1)S(1)} %get-tuple-element.15), channel_id=1, source_target_pairs={{0,20},{1,21},{2,22},{3,23},{4,16},{5,17},{6,18},{7,19},{8,28},{9,... | collective-permute-start | bytes 1572872 | tf_op jit(solution)/shard_map/ppermute | solution.py:271
  596.2 98.9 %collective-permute-start.52 = (bf16[64,16,256]{2,0,1:T(8,128)(2,1)S(1)}, bf16[64,16,256]{2,0,1:T(8,128)(2,1)S(1)}, u32[]{:S(2)}, u32[]{:S(2)}) collective-permute-start(bf16[64,16,256]{2,0,1:T(8,128)(2,1)S(1)} %get-tuple-element.16), channel_id=1, source_target_pairs={{0,16},{1,17},{2,18},{3,19},{4,20},{5,21},{6,22},{7,23},{8,24},{9,... | collective-permute-start | bytes 1572872 | tf_op jit(solution)/shard_map/ppermute | solution.py:271
  598.9 90.8 %collective-permute-start.18 = (bf16[64,16,128]{2,0,1:T(8,128)(2,1)S(1)}, bf16[64,16,128]{2,0,1:T(8,128)(2,1)S(1)}, u32[]{:S(2)}, u32[]{:S(2)}) collective-permute-start(bf16[64,16,128]{2,0,1:T(8,128)(2,1)S(1)} %get-tuple-element.47), channel_id=1, source_target_pairs={{0,20},{1,21},{2,22},{3,23},{4,16},{5,17},{6,18},{7,19},{8,28},{9,... | collective-permute-start | bytes 786440 | tf_op jit(solution)/shard_map/ppermute | solution.py:271
  695.1 48.9 %collective-permute-start.33 = (bf16[64,16,256]{2,0,1:T(8,128)(2,1)S(1)}, bf16[64,16,256]{2,0,1:T(8,128)(2,1)S(1)}, u32[]{:S(2)}, u32[]{:S(2)}) collective-permute-start(bf16[64,16,256]{2,0,1:T(8,128)(2,1)S(1)} %get-tuple-element.22), channel_id=1, source_target_pairs={{0,24},{1,25},{2,26},{3,27},{4,28},{5,29},{6,30},{7,31},{8,16},{9,... | collective-permute-start | bytes 1572872 | tf_op jit(solution)/shard_map/ppermute | solution.py:271
  707.2 74.3 %collective-permute-start.32 = (bf16[64,16,256]{2,0,1:T(8,128)(2,1)S(1)}, bf16[64,16,256]{2,0,1:T(8,128)(2,1)S(1)}, u32[]{:S(2)}, u32[]{:S(2)}) collective-permute-start(bf16[64,16,256]{2,0,1:T(8,128)(2,1)S(1)} %get-tuple-element.23), channel_id=1, source_target_pairs={{0,20},{1,21},{2,22},{3,23},{4,16},{5,17},{6,18},{7,19},{8,28},{9,... | collective-permute-start | bytes 1572872 | tf_op jit(solution)/shard_map/ppermute | solution.py:271
  718.4 73.5 %collective-permute-start.31 = (bf16[64,16,256]{2,0,1:T(8,128)(2,1)S(1)}, bf16[64,16,256]{2,0,1:T(8,128)(2,1)S(1)}, u32[]{:S(2)}, u32[]{:S(2)}) collective-permute-start(bf16[64,16,256]{2,0,1:T(8,128)(2,1)S(1)} %get-tuple-element.24), channel_id=1, source_target_pairs={{0,16},{1,17},{2,18},{3,19},{4,20},{5,21},{6,22},{7,23},{8,24},{9,... | collective-permute-start | bytes 1572872 | tf_op jit(solution)/shard_map/ppermute | solution.py:271
  722.0 70.2 %collective-permute-start.30 = (bf16[64,16,256]{2,0,1:T(8,128)(2,1)S(1)}, bf16[64,16,256]{2,0,1:T(8,128)(2,1)S(1)}, u32[]{:S(2)}, u32[]{:S(2)}) collective-permute-start(bf16[64,16,256]{2,0,1:T(8,128)(2,1)S(1)} %get-tuple-element.25), channel_id=1, source_target_pairs={{0,12},{1,13},{2,14},{3,15},{4,8},{5,9},{6,10},{7,11},{8,4},{9,5},... | collective-permute-start | bytes 1572872 | tf_op jit(solution)/shard_map/ppermute | solution.py:271
  731.4 61.1 %collective-permute-start.29 = (bf16[64,16,256]{2,0,1:T(8,128)(2,1)S(1)}, bf16[64,16,256]{2,0,1:T(8,128)(2,1)S(1)}, u32[]{:S(2)}, u32[]{:S(2)}) collective-permute-start(bf16[64,16,256]{2,0,1:T(8,128)(2,1)S(1)} %get-tuple-element.26), channel_id=1, source_target_pairs={{0,8},{1,9},{2,10},{3,11},{4,12},{5,13},{6,14},{7,15},{8,0},{9,1},... | collective-permute-start | bytes 1572872 | tf_op jit(solution)/shard_map/ppermute | solution.py:271
  744.0 48.8 %collective-permute-start.28 = (bf16[64,16,256]{2,0,1:T(8,128)(2,1)S(1)}, bf16[64,16,256]{2,0,1:T(8,128)(2,1)S(1)}, u32[]{:S(2)}, u32[]{:S(2)}) collective-permute-start(bf16[64,16,256]{2,0,1:T(8,128)(2,1)S(1)} %get-tuple-element.27), channel_id=1, source_target_pairs={{0,4},{1,5},{2,6},{3,7},{4,0},{5,1},{6,2},{7,3},{8,12},{9,13},{10,... | collective-permute-start | bytes 1572872 | tf_op jit(solution)/shard_map/ppermute | solution.py:271
  (72 other events, 1493.5 us)
Sparse Core Ops, SparseCore 0:
  8.9 202.2 all-gather.2
  212.8 201.5 all-gather.4

commit v3 on v2

v3 whole, which is shorter than its diff:
```python
import functools

import jax
import jax.numpy as jnp
from jax import lax
from jax.experimental import pallas as pl
from jax.experimental.layout import Layout, with_layout_constraint
from jax.experimental.pallas import tpu as pltpu
from jax.sharding import PartitionSpec as P

LX = 16
LY = 16
DRIVE = 128


U_BASE = 4.0
TIME_STEP = 0.02

FAR_WINDOW = 2
NEAR_WINDOW = 2
VMEM_BYTES = 56 * 1024 * 1024


def lattice_tables(momentum_ids):
    momenta = momentum_ids.shape[0]
    wave_x = momentum_ids // LY
    wave_y = momentum_ids % LY
    sites = jnp.arange(momenta, dtype=jnp.int32)
    site_x = sites // LY
    site_y = sites % LY
    phase = (
        wave_x[:, None] * site_x[None, :] % LX * LY + wave_y[:, None] * site_y[None, :] % LY * LX
    )
    angle = 2.0 * jnp.pi / momenta * (phase % momenta).astype(jnp.float32)
    return (jnp.cos(angle), jnp.sin(angle), momenta)


def transforms(momentum_ids, groups):
    cos_table, sin_table, momenta = lattice_tables(momentum_ids)
    local_k = momenta // groups
    forward = jnp.stack(
        [jnp.stack([cos_table, sin_table], 1), jnp.stack([-sin_table, cos_table], 1)], 0
    )
    forward = (forward / momenta).astype(jnp.bfloat16)
    forward = forward.reshape(2, groups, local_k, 2, momenta).transpose(3, 4, 1, 0, 2)
    backward = jnp.stack(
        [jnp.stack([cos_table.T, -sin_table.T], 1), jnp.stack([sin_table.T, cos_table.T], 1)], 0
    ).astype(jnp.bfloat16)
    backward = backward.reshape(2, momenta, 2, groups, local_k).transpose(3, 2, 4, 0, 1)
    return (
        forward.reshape(2 * momenta, 2 * momenta),
        backward.reshape(2 * momenta, 2 * momenta),
    )


def drive(window_start, row_times):
    phase = ((window_start[0] + row_times) % DRIVE).astype(jnp.float32)
    return U_BASE * (1.0 + 0.5 * jnp.sin(2.0 * jnp.pi / DRIVE * phase))


def born_kernel(pieces, order_ref, *refs):
    x_refs = refs[:pieces]
    forward_ref, backward_ref, weight_ref, mask_ref, out_ref = refs[pieces:]
    half = forward_ref.shape[0] // 2
    table = forward_ref[...]
    weight = -weight_ref[0]
    less = jnp.dot(
        table,
        jnp.concatenate([ref[0, 0] for ref in x_refs], axis=0),
        preferred_element_type=jnp.float32,
    )
    more = jnp.dot(
        table,
        jnp.concatenate([ref[0, 1] for ref in x_refs], axis=0),
        preferred_element_type=jnp.float32,
    )
    less_re, less_im = (less[:half], less[half:])
    more_re, more_im = (more[:half], more[half:])
    square_re = less_re * less_re - less_im * less_im
    square_im = 2.0 * less_re * less_im
    sigma_less = jnp.concatenate(
        [
            (weight * (square_re * more_re + square_im * more_im)).astype(jnp.bfloat16),
            (weight * (square_im * more_re - square_re * more_im)).astype(jnp.bfloat16),
        ],
        axis=0,
    )
    other_re = more_re * more_re - more_im * more_im
    other_im = 2.0 * more_re * more_im
    sigma_more = jnp.concatenate(
        [
            (weight * (other_re * less_re + other_im * less_im)).astype(jnp.bfloat16),
            (weight * (other_im * less_re - other_re * less_im)).astype(jnp.bfloat16),
        ],
        axis=0,
    )
    back = backward_ref[...]
    less_mom = jnp.dot(back, sigma_less, preferred_element_type=jnp.float32)
    more_mom = jnp.dot(back, sigma_more, preferred_element_type=jnp.float32)
    ret = (mask_ref[0] * (more_mom - less_mom)).astype(jnp.bfloat16)
    _, _, _, depth, width = out_ref.shape
    kinds = (less_mom.astype(jnp.bfloat16), ret)
    for piece in range(pieces):
        for kind in range(2):
            rows = kinds[kind][piece * depth : (piece + 1) * depth]
            out_ref[order_ref[piece], kind, 0] = rows


def born(order, spread, forward, backward, weight, mask):
    pieces = len(spread)
    sub_rows, _, depth, width = spread[0].shape
    size = pieces * depth
    out_shape = (pieces, 2, sub_rows, depth, width)
    grid_spec = pltpu.PrefetchScalarGridSpec(
        num_scalar_prefetch=1,
        grid=(sub_rows,),
        in_specs=[pl.BlockSpec((1, 2, depth, width), lambda i, order: (i, 0, 0, 0))] * pieces
        + [
            pl.BlockSpec((size, size), lambda i, order: (0, 0)),
            pl.BlockSpec((size, size), lambda i, order: (0, 0)),
            pl.BlockSpec((1, 1, width), lambda i, order: (i, 0, 0)),
            pl.BlockSpec((1, 1, width), lambda i, order: (i, 0, 0)),
        ],
        out_specs=pl.BlockSpec(
            (pieces, 2, 1, depth, width), lambda i, order: (0, 0, i, 0, 0)
        ),
    )
    return pl.pallas_call(
        functools.partial(born_kernel, pieces),
        grid_spec=grid_spec,
        out_shape=jax.ShapeDtypeStruct(out_shape, jnp.bfloat16),
        compiler_params=pltpu.CompilerParams(vmem_limit_bytes=VMEM_BYTES),
        cost_estimate=pl.CostEstimate(
            flops=8 * size * size * sub_rows * width,
            bytes_accessed=8 * size * sub_rows * width,
            transcendentals=0,
        ),
        name="born",
    )(order, *spread, forward, backward, weight, mask)


def sigma_rows(ref, kind, part, index, order_ref):
    if order_ref is None:
        value = ref[:, kind, part, index]
    else:
        places = range(ref.shape[0])
        value = jnp.stack([ref[order_ref[place], kind, part, index] for place in places])
    return value.reshape(value.shape[0] * value.shape[1], value.shape[2])


def complex_left(terms, index, order_ref):
    re = [sigma_rows(ref, kind, 0, index, order_ref) for ref, kind in terms]
    im = [sigma_rows(ref, kind, 1, index, order_ref) for ref, kind in terms]
    top, low = (re + [-v for v in im], im + re)
    return jnp.concatenate(
        [jnp.concatenate(top, axis=1), jnp.concatenate(low, axis=1)], axis=0
    )


def collide_kernel(plan, order_ref, *refs):
    count, ret_terms, less_terms, first_col, gap_step, gap_col, has_total, has_old, has_rest, mixed = plan
    order_ref = order_ref if mixed else None
    refs = list(refs)
    sources = [refs.pop(0) for _ in range(count)]
    lesser_ref = refs.pop(0) if ret_terms else None
    gap_less_ref, gap_more_ref = (refs.pop(0), refs.pop(0))
    total_ref = refs.pop(0) if has_total else None
    if has_old:
        refs.pop(0)
    out_ref = refs.pop(0) if not has_rest or len(refs) == 2 else None
    rest_ref = refs.pop(0) if has_rest else None
    block, steps, gap_cols = gap_less_ref.shape[1:]
    rows = sources[0].shape[0] * sources[0].shape[4]
    done_cols = out_ref.shape[3] if out_ref is not None else 0
    shape = (steps, gap_cols)
    step_index = gap_step + lax.broadcasted_iota(jnp.int32, shape, 0)
    upper = step_index <= gap_col + lax.broadcasted_iota(jnp.int32, shape, 1)
    ret_terms = [(sources[source], kind) for source, kind in ret_terms]
    less_terms = [(sources[source], kind) for source, kind in less_terms]
    for index in range(block):

        def advanced(part):
            gap = gap_less_ref[part, index].astype(jnp.float32)
            gap = gap - gap_more_ref[part, index].astype(jnp.float32)
            return jnp.where(upper, gap, 0.0).astype(jnp.bfloat16)

        def product(left, *right):
            return jnp.dot(
                left, jnp.concatenate(right, axis=0), preferred_element_type=jnp.float32
            )

        left = complex_left(less_terms, index, order_ref)
        if not ret_terms:
            value = product(left, advanced(0), advanced(1))
        elif gap_col == first_col:
            value = product(
                jnp.concatenate([left, complex_left(ret_terms, index, order_ref)], axis=1),
                advanced(0),
                advanced(1),
                lesser_ref[0, index],
                lesser_ref[1, index],
            )
        else:
            value = product(
                complex_left(ret_terms, index, order_ref), lesser_ref[0, index], lesser_ref[1, index]
            )
            skipped = gap_col - first_col
            value = jnp.concatenate(
                [
                    value[:, :skipped],
                    value[:, skipped:] + product(left, advanced(0), advanced(1)),
                ],
                axis=1,
            )
        for part in range(2):
            one = value[part * rows : (part + 1) * rows]
            if has_total:
                one = total_ref[part, index] + one
            if out_ref is not None:
                out_ref[part, index] = (TIME_STEP * one[:, :done_cols]).astype(out_ref.dtype)
            if rest_ref is not None:
                rest_ref[part, index] = one[:, done_cols:]


def collide(order, sources, ret, less, functions, carried, cols, block, mixed=False):
    ret_terms, ret_step, ret_steps = ret
    less_terms, gap_step, gap_steps, gap_col = less
    less_all, more_all = functions
    first_col, last_col = cols
    total, output = carried
    _, local_k, _, col_count = less_all.shape
    rows = sources[0].shape[0] * sources[0].shape[4]
    span = col_count - first_col
    block = min(block, local_k)
    done_cols = last_col - first_col
    arrays, specs = ([], [])

    def take(array, shape, *place):
        arrays.append(array)
        specs.append(pl.BlockSpec(shape, lambda k, order: (0, k, *place)))

    for array in sources:
        count, kinds, _, _, sub_rows, width = array.shape
        arrays.append(array)
        specs.append(
            pl.BlockSpec(
                (count, kinds, 2, block, sub_rows, width), lambda k, order: (0, 0, 0, k, 0, 0)
            )
        )
    if ret_terms:
        take(less_all, (2, block, ret_steps, span), ret_step // ret_steps, first_col // span)
    gap_span = col_count - gap_col
    for array in (less_all, more_all):
        take(array, (2, block, gap_steps, gap_span), gap_step // gap_steps, gap_col // gap_span)
    if total is not None:
        take(total, (2, block, rows, span), 0, 0)
    out_specs, out_shape, aliases = ([], [], {})
    if done_cols:
        if output is not None:
            arrays.append(output)
            specs.append(pl.BlockSpec(memory_space=pl.ANY))
            aliases = {len(arrays): 0}
        out_specs.append(
            pl.BlockSpec(
                (2, block, rows, done_cols), lambda k, order: (0, k, 0, first_col // done_cols)
            )
        )
        out_shape.append(jax.ShapeDtypeStruct((2, local_k, rows, col_count), jnp.bfloat16))
    has_rest = last_col < col_count
    if has_rest:
        rest = col_count - last_col
        out_specs.append(pl.BlockSpec((2, block, rows, rest), lambda k, order: (0, k, 0, 0)))
        out_shape.append(jax.ShapeDtypeStruct((2, local_k, rows, rest), jnp.float32))
    plan = (
        len(sources),
        ret_terms,
        less_terms,
        first_col,
        gap_step,
        gap_col,
        total is not None,
        bool(aliases),
        has_rest,
        mixed,
    )
    work = ret_steps * span + gap_steps * gap_span
    results = list(
        pl.pallas_call(
            functools.partial(collide_kernel, plan),
            grid_spec=pltpu.PrefetchScalarGridSpec(
                num_scalar_prefetch=1, grid=(local_k // block,), in_specs=specs, out_specs=out_specs
            ),
            out_shape=out_shape,
            input_output_aliases=aliases,
            compiler_params=pltpu.CompilerParams(vmem_limit_bytes=VMEM_BYTES),
            cost_estimate=pl.CostEstimate(
                flops=8 * local_k * rows * work,
                bytes_accessed=12 * local_k * work + 8 * local_k * rows * span,
                transcendentals=0,
            ),
            name="collide",
        )(order, *arrays)
    )
    output = results.pop(0) if done_cols else None
    return (results.pop(0) if has_rest else None, output)


def on_device(lesser, greater, momentum_ids, window_start):
    _, local_k, row_count, col_count = lesser.shape
    groups, ranks = (lax.axis_size("mom"), lax.axis_size("trow"))
    group = lax.axis_index("mom")
    sub_rows = row_count // groups
    depth = 2 * local_k
    order = group ^ jnp.arange(groups, dtype=jnp.int32)
    far, near = (list(range(groups // 2, groups)), list(range(1, groups // 2)))
    offsets = [d for pair in zip(far, near + [0]) for d in pair if d]
    arrived = {True: [], False: []}

    def send(make, arrays, offset):
        is_far = 2 * offset >= groups
        queue, ahead = (arrived[is_far], FAR_WINDOW if is_far else NEAR_WINDOW)
        if len(queue) >= ahead:
            arrays, _ = lax.optimization_barrier((arrays, queue[-ahead]))
        pairs = [(g * ranks + r, (g ^ offset) * ranks + r) for g in range(groups) for r in range(ranks)]
        queue.append(lax.ppermute(make(*arrays), ("mom", "trow"), pairs))
        return queue[-1]

    def pack(offset, first, count, arrays):
        def rows_of(array):
            return lax.dynamic_slice(
                array,
                (0, 0, (group ^ offset) * sub_rows, first),
                (2, local_k, sub_rows, count),
            )

        both = jnp.stack([rows_of(array) for array in arrays])
        return both.transpose(3, 0, 1, 2, 4).reshape(sub_rows, 2, depth, count)

    width = col_count // 4
    halves = [(0, 3 * width), (3 * width, width)]
    row_first = lax.axis_index("trow") * row_count + group * sub_rows
    row_times = row_first + jnp.arange(sub_rows, dtype=jnp.int32)
    spreads = []
    for first, count in halves:
        spread = {0: pack(0, first, count, (lesser, greater))}
        for d in offsets:
            spread[d] = send(
                lambda *arrays: pack(d, first, count, arrays), (lesser, greater), d
            )
        spreads.append([spread[d] for d in range(groups)])

    functions = tuple(
        lax.all_gather(array, "trow", axis=2, tiled=True) for array in (lesser, greater)
    )
    forward, backward = transforms(
        momentum_ids.reshape(groups, local_k)[order].reshape(-1), groups
    )
    row_drive = drive(window_start, row_times)

    def born_part(part, before=None):
        first, count = halves[part]
        col_index = first + jnp.arange(count, dtype=jnp.int32)
        weight = row_drive[:, None] * drive(window_start, col_index)[None, :]
        mask = (row_times[:, None] >= col_index[None, :]).astype(jnp.float32)
        if before is not None:
            weight, _ = lax.optimization_barrier((weight, before))
        sigma = born(order, spreads[part], forward, backward, weight[:, None], mask[:, None])
        return with_layout_constraint(sigma.transpose(0, 1, 3, 2, 4), Layout((0, 1, 2, 3, 4)))

    def exchange(make, sigma, before=None, before_last=None):
        got = {}
        for d in offsets:
            after = before_last if d == far[-1] and before_last is not None else before
            held = sigma
            if after is not None:
                held, _ = lax.optimization_barrier((sigma, after))
            got[d] = send(lambda array: make(array[group ^ d]), (held,), d)
        got[0] = make(sigma[group])
        got = jnp.stack([got[d] for d in range(groups)])
        kinds, count = (got.shape[1], got.shape[4])
        got = got.reshape(groups, kinds, 2, local_k, sub_rows, count)
        if sub_rows % 16 == 0:
            return got
        got = got[order].transpose(1, 2, 3, 0, 4, 5)
        return got.reshape(1, kinds, 2, local_k, groups * sub_rows, count)

    mixed = sub_rows % 16 == 0
    sigma = born_part(0)
    low = exchange(lambda array: array, sigma)
    low_total, _ = collide(
        order,
        [low],
        ([(0, 1)], 0, 3 * width),
        ([(0, 0)], 0, 3 * width, 0),
        functions,
        (None, None),
        (0, 0),
        2,
        mixed,
    )
    sigma = born_part(1)
    high = exchange(lambda array: array, sigma, None, low_total)
    _, output = collide(
        order,
        [high],
        ([(0, 1)], 3 * width, width),
        ([(0, 0)], 3 * width, width, 3 * width),
        functions,
        (low_total, None),
        (0, col_count),
        4,
        mixed,
    )
    return output


def solution(mesh):
    return jax.shard_map(
        on_device,
        mesh=mesh,
        in_specs=(P(None, "mom", "trow", None), P(None, "mom", "trow", None), P(), P()),
        out_specs=P(None, "mom", "trow", None),
        check_vma=False,
    )
```

time: 880 us -> 793 us (0.901)
  the two profiles are of different devices: /device:TPU:7 before, /device:TPU:0 now
where the time goes in v3:
time: 793 us; the launch traced here: 791 us
  waiting for transfers between devices  349 us (44%)
  starting transfers between devices  226 us (28%)
  Pallas kernels  102 us (13%)
  local copies, waits for them, and re-layouts  91.3 us (12%)
  between operations  14.7 us (2%)
  other arithmetic  8.42 us (1%)
    ppermute x28, waiting for transfers between devices, send(): queue.append(lax.ppermute(make(*arrays), ('mom', 'trow'), pairs))  347 us
    ppermute x28, starting transfers between devices, send(): queue.append(lax.ppermute(make(*arrays), ('mom', 'trow'), pairs))  226 us
    pallas_call x2, Pallas kernels, collide(): pl.pallas_call(functools.partial(collide_kernel, plan), grid_spec=pltpu.P...  55.4 us
    pallas_call x2, Pallas kernels, born(): pl.pallas_call(functools.partial(born_kernel, pieces), grid_spec=grid_spe...  46.5 us
    another operation x20, local copies, waits for them, and re-layouts, pack(): both = jnp.stack([rows_of(array) for array in arrays])  26.9 us
    pallas_call x2, local copies, waits for them, and re-layouts, born(): pl.pallas_call(functools.partial(born_kernel, pieces), grid_spec=grid_spe...  18.4 us
    squeeze x14, local copies, waits for them, and re-layouts, exchange(): got[d] = send(lambda array: make(array[group ^ d]), (held,), d)  16.3 us
  transfers between devices with their start and end apart: 30, of which 9 were waited for; matrix products, arithmetic and copies ran while one was open for 12% of the time, Pallas kernels for 11%

profile of v3, /device:TPU:0, one launch (start us, length us, event | category | flops | bytes accessed | tf_op | source)
XLA Modules:
  0.0 790.7 jit_solution(12496007350170474025)
XLA Ops:
  8.0 2.6 dynamic-slice_bitcast_fusion.7
  10.6 2.6 dynamic-slice_bitcast_fusion.8
  14.9 3.0 collective-permute-start
  22.9 2.6 collective-permute-start.6
  38.6 42.9 %collective-permute-done.refs_2_ = bf16[16,2,64,384]{3,2,1,0:T(8,128)(2,1)} collective-permute-done((bf16[16,2,64,384]{3,2,1,0:T(8,128)(2,1)}, bf16[16,2,64,384]{3,2,1,0:T(8,128)(2,1)}, u32[]{:S(2)}, u32[]{:S(2)}) %collective-permute-start) | collective-permute-done | bytes 1572896 | tf_op jit(solution)/shard_map/ppermute | solution.py:325
  86.3 42.6 %collective-permute-done.6.refs_4_ = bf16[16,2,64,384]{3,2,1,0:T(8,128)(2,1)} collective-permute-done((bf16[16,2,64,384]{3,2,1,0:T(8,128)(2,1)}, bf16[16,2,64,384]{3,2,1,0:T(8,128)(2,1)}, u32[]{:S(2)}, u32[]{:S(2)}) %collective-permute-start.6) | collective-permute-done | bytes 1572896 | tf_op jit(solution)/shard_map/ppermute | solution.py:325
  131.9 2.7 collective-permute-start.7
  134.6 61.7 %collective-permute-done.9.refs_5_ = bf16[16,2,64,384]{3,2,1,0:T(8,128)(2,1)} collective-permute-done((bf16[16,2,64,384]{3,2,1,0:T(8,128)(2,1)}, bf16[16,2,64,384]{3,2,1,0:T(8,128)(2,1)}, u32[]{:S(2)}, u32[]{:S(2)}) %collective-permute-start.9) | collective-permute-done | bytes 1572896 | tf_op jit(solution)/shard_map/ppermute | solution.py:325
  199.3 3.5 collective-permute-start.10
  206.1 40.3 %collective-permute-done.1.refs_1_ = bf16[16,2,64,128]{3,2,1,0:T(8,128)(2,1)S(1)} collective-permute-done((bf16[16,2,64,128]{3,2,1,0:T(8,128)(2,1)S(1)}, bf16[16,2,64,128]{3,2,1,0:T(8,128)(2,1)S(1)}, u32[]{:S(2)}, u32[]{:S(2)}) %collective-permute-start.1) | collective-permute-done | bytes 524320 | tf_op jit(solution)/shard_map/ppermute | solution.py:325
  250.6 3.0 collective-permute-start.4
  255.3 11.7 %collective-permute-start.8 = (bf16[16,2,64,128]{3,2,1,0:T(8,128)(2,1)S(1)}, bf16[16,2,64,128]{3,2,1,0:T(8,128)(2,1)S(1)}, u32[]{:S(2)}, u32[]{:S(2)}) collective-permute-start(bf16[16,2,64,128]{3,2,1,0:T(8,128)(2,1)S(1)} %bitcast.222), channel_id=1, source_target_pairs={{0,16},{1,17},{2,18},{3,19},{4,20},{5,21},{6,22},{7,23},{8,24},{9,... | collective-permute-start | bytes 1572872 | tf_op jit(solution)/shard_map/ppermute | solution.py:325
  268.7 44.7 %collective-permute-start.11 = (bf16[16,2,64,128]{3,2,1,0:T(8,128)(2,1)S(1)}, bf16[16,2,64,128]{3,2,1,0:T(8,128)(2,1)S(1)}, u32[]{:S(2)}, u32[]{:S(2)}) collective-permute-start(bf16[16,2,64,128]{3,2,1,0:T(8,128)(2,1)S(1)} %bitcast.221), channel_id=1, source_target_pairs={{0,20},{1,21},{2,22},{3,23},{4,16},{5,17},{6,18},{7,19},{8,28},{9,... | collective-permute-start | bytes 1572872 | tf_op jit(solution)/shard_map/ppermute | solution.py:325
  313.4 28.5 %born.3 = bf16[8,2,16,64,384]{4,3,2,1,0:T(8,128)(2,1)} custom-call(s32[8]{0:T(128)} %iota_xor_fusion.order_ref, bf16[16,2,64,384]{3,2,1,0:T(8,128)(2,1)} %bitcast.202, bf16[16,2,64,384]{3,2,1,0:T(8,128)(2,1)} %collective-permute-done.2.refs_1_, bf16[16,2,64,384]{3,2,1,0:T(8,128)(2,1)} %collective-permute-done.refs_2_, bf16[16,2,64,384]{3,2,1,0:T(8,128)(2,1)} %copy-done.4, ...), custom_call_target="tpu_custom_call" | custom-call | flops 12884901888 | bytes 25165824 | tf_op jit(solution)/shard_map/born/pallas_call | solution.py:128
  341.9 12.7 %copy.54 = bf16[8,2,16,64,384]{4,2,3,1,0:T(8,128)(2,1)S(1)} copy(bf16[8,2,16,64,384]{4,3,2,1,0:T(8,128)(2,1)} %born.3) | data formatting | bytes 25165824 | tf_op jit(solution)/shard_map/born/pallas_call | solution.py:128
  368.8 5.4 collective-permute-done.12.refs_6_
  375.5 18.3 %collective-permute-start.20 = (bf16[2,64,16,384]{3,2,1,0:T(8,128)(2,1)}, bf16[2,64,16,384]{3,2,1,0:T(8,128)(2,1)}, u32[]{:S(2)}, u32[]{:S(2)}) collective-permute-start(bf16[2,64,16,384]{3,2,1,0:T(8,128)(2,1)} %dynamic-slice_bitcast_fusion.3), channel_id=1, source_target_pairs={{0,16},{1,17},{2,18},{3,19},{4,20},{5,21},{6,22},{7,23},{8,24},{9,... | collective-permute-start | bytes 4718600 | tf_op jit(solution)/shard_map/ppermute | solution.py:325
  393.9 2.7 dynamic-slice_bitcast_fusion.1
  396.6 10.9 %collective-permute-start.23 = (bf16[2,64,16,384]{3,2,1,0:T(8,128)(2,1)}, bf16[2,64,16,384]{3,2,1,0:T(8,128)(2,1)}, u32[]{:S(2)}, u32[]{:S(2)}) collective-permute-start(bf16[2,64,16,384]{3,2,1,0:T(8,128)(2,1)} %dynamic-slice_bitcast_fusion.1), channel_id=1, source_target_pairs={{0,20},{1,21},{2,22},{3,23},{4,16},{5,17},{6,18},{7,19},{8,28},{9,... | collective-permute-start | bytes 4718600 | tf_op jit(solution)/shard_map/ppermute | solution.py:325
  411.4 2.7 dynamic-slice_bitcast_fusion.4
  414.3 18.0 %born.2 = bf16[8,2,16,64,128]{4,3,2,1,0:T(8,128)(2,1)} custom-call(s32[8]{0:T(128)} %iota_xor_fusion.order_ref, bf16[16,2,64,128]{3,2,1,0:T(8,128)(2,1)} %bitcast.218, bf16[16,2,64,128]{3,2,1,0:T(8,128)(2,1)} %copy-done.7, bf16[16,2,64,128]{3,2,1,0:T(8,128)(2,1)} %collective-permute-done.4.refs_2_, bf16[16,2,64,128]{3,2,1,0:T(8,128)(2,1)} %collective-permute-done.5.refs_3_, ...), custom_call_target="tpu_custom_call" | custom-call | flops 4294967296 | bytes 8388608 | tf_op jit(solution)/shard_map/born/pallas_call | solution.py:128
  432.3 5.7 copy.55
  438.0 66.6 %collective-permute-done.20 = bf16[2,64,16,384]{3,2,1,0:T(8,128)(2,1)} collective-permute-done((bf16[2,64,16,384]{3,2,1,0:T(8,128)(2,1)}, bf16[2,64,16,384]{3,2,1,0:T(8,128)(2,1)}, u32[]{:S(2)}, u32[]{:S(2)}) %collective-permute-start.20) | collective-permute-done | bytes 1572896 | tf_op jit(solution)/shard_map/ppermute | solution.py:325
  509.2 62.9 %collective-permute-done.23 = bf16[2,64,16,384]{3,2,1,0:T(8,128)(2,1)} collective-permute-done((bf16[2,64,16,384]{3,2,1,0:T(8,128)(2,1)}, bf16[2,64,16,384]{3,2,1,0:T(8,128)(2,1)}, u32[]{:S(2)}, u32[]{:S(2)}) %collective-permute-start.23) | collective-permute-done | bytes 1572896 | tf_op jit(solution)/shard_map/ppermute | solution.py:325
  580.8 3.0 collective-permute-start.18
  585.8 59.6 %collective-permute-start.22 = (bf16[2,64,16,128]{3,2,1,0:T(8,128)(2,1)S(1)}, bf16[2,64,16,128]{3,2,1,0:T(8,128)(2,1)S(1)}, u32[]{:S(2)}, u32[]{:S(2)}) collective-permute-start(bf16[2,64,16,128]{3,2,1,0:T(8,128)(2,1)S(1)} %dynamic-slice_bitcast_fusion.26), channel_id=1, source_target_pairs={{0,16},{1,17},{2,18},{3,19},{4,20},{5,21},{6,22},{7,23},{8,24},{9,... | collective-permute-start | bytes 1572872 | tf_op jit(solution)/shard_map/ppermute | solution.py:325
  648.1 44.0 %collective-permute-start.25 = (bf16[2,64,16,128]{3,2,1,0:T(8,128)(2,1)}, bf16[2,64,16,128]{3,2,1,0:T(8,128)(2,1)S(1)}, u32[]{:S(2)}, u32[]{:S(2)}) collective-permute-start(bf16[2,64,16,128]{3,2,1,0:T(8,128)(2,1)} %dynamic-slice_bitcast_fusion.25), channel_id=1, source_target_pairs={{0,20},{1,21},{2,22},{3,23},{4,16},{5,17},{6,18},{7,19},{8,28},{9,... | collective-permute-start | bytes 1572872 | tf_op jit(solution)/shard_map/ppermute | solution.py:325
  692.7 19.6 %collective-permute-done.22 = bf16[2,64,16,128]{3,2,1,0:T(8,128)(2,1)S(1)} collective-permute-done((bf16[2,64,16,128]{3,2,1,0:T(8,128)(2,1)S(1)}, bf16[2,64,16,128]{3,2,1,0:T(8,128)(2,1)S(1)}, u32[]{:S(2)}, u32[]{:S(2)}) %collective-permute-start.22) | collective-permute-done | bytes 524320 | tf_op jit(solution)/shard_map/ppermute | solution.py:325
  714.5 38.4 %collide.2.refs_4_ = f32[2,32,128,512]{3,2,1,0:T(8,128)} custom-call(s32[8]{0:T(128)} %iota_xor_fusion.order_ref, bf16[8,2,2,32,16,384]{5,4,3,2,1,0:T(8,128)(2,1)} %copy-done.2, bf16[2,32,512,512]{3,2,1,0:T(8,128)(2,1)} %all-gather.3.cloned.1.call-done.refs_1_.refs_2_, bf16[2,32,512,512]{3,2,1,0:T(8,128)(2,1)} %all-gather.3.cloned.1.call-done.refs_1_.refs_2_, ...), custom_call_target="tpu_custom_call" | custom-call | flops 12884901888 | bytes 167772160 | tf_op jit(solution)/shard_map/collide/pallas_call | solution.py:288
  754.0 2.6 collective-permute-start.27
  760.9 5.2 collective-permute-done.27
  766.9 17.0 %collide.3 = bf16[2,32,128,512]{3,2,1,0:T(8,128)(2,1)} custom-call(s32[8]{0:T(128)} %iota_xor_fusion.order_ref, bf16[8,2,2,32,16,128]{5,4,3,2,1,0:T(8,128)(2,1)} %constant_dynamic-update-slice_fusion.8.refs_0_, bf16[2,32,512,512]{3,2,1,0:T(8,128)(2,1)} %all-gather.3.cloned.1.call-done.refs_1_.refs_2_, ...), custom_call_target="tpu_custom_call" | custom-call | flops 2684354560 | bytes 48234496 | tf_op jit(solution)/shard_map/collide/pallas_call | solution.py:288
  (168 shorter events, 88.5 us)
Async XLA Ops:
  6.5 708.0 %all-gather.3.cloned.1.call-start = ((), (), s32[]{:S(2)}) async-start(), calls=%async_computation | async-start | bytes 41943040 | tf_op jit(solution)/shard_map/all_gather | solution.py:353
  7.3 707.3 %all-gather.5.cloned.1.call-start = ((), (), s32[]{:S(2)}) async-start(), calls=%async_computation.1 | async-start | bytes 41943040 | tf_op jit(solution)/shard_map/all_gather | solution.py:353
  14.9 66.6 %collective-permute-start = (bf16[16,2,64,384]{3,2,1,0:T(8,128)(2,1)}, bf16[16,2,64,384]{3,2,1,0:T(8,128)(2,1)}, u32[]{:S(2)}, u32[]{:S(2)}) collective-permute-start(bf16[16,2,64,384]{3,2,1,0:T(8,128)(2,1)} %bitcast.7), channel_id=1, source_target_pairs={{0,8},{1,9},{2,10},{3,11},{4,12},{5,13},{6,14},{7,15},{8,0},{9,1},... | collective-permute-start | bytes 4718600 | tf_op jit(solution)/shard_map/ppermute | solution.py:325
  19.7 61.9 %collective-permute-start.2 = (bf16[16,2,64,384]{3,2,1,0:T(8,128)(2,1)}, bf16[16,2,64,384]{3,2,1,0:T(8,128)(2,1)}, u32[]{:S(2)}, u32[]{:S(2)}) collective-permute-start(bf16[16,2,64,384]{3,2,1,0:T(8,128)(2,1)} %bitcast.15), channel_id=1, source_target_pairs={{0,4},{1,5},{2,6},{3,7},{4,0},{5,1},{6,2},{7,3},{8,12},{9,13},{10,... | collective-permute-start | bytes 4718600 | tf_op jit(solution)/shard_map/ppermute | solution.py:325
  22.9 106.0 %collective-permute-start.6 = (bf16[16,2,64,384]{3,2,1,0:T(8,128)(2,1)}, bf16[16,2,64,384]{3,2,1,0:T(8,128)(2,1)}, u32[]{:S(2)}, u32[]{:S(2)}) collective-permute-start(bf16[16,2,64,384]{3,2,1,0:T(8,128)(2,1)} %bitcast.31), channel_id=1, source_target_pairs={{0,16},{1,17},{2,18},{3,19},{4,20},{5,21},{6,22},{7,23},{8,24},{9,... | collective-permute-start | bytes 4718600 | tf_op jit(solution)/shard_map/ppermute | solution.py:325
  27.2 169.1 %collective-permute-start.9 = (bf16[16,2,64,384]{3,2,1,0:T(8,128)(2,1)}, bf16[16,2,64,384]{3,2,1,0:T(8,128)(2,1)}, u32[]{:S(2)}, u32[]{:S(2)}) collective-permute-start(bf16[16,2,64,384]{3,2,1,0:T(8,128)(2,1)} %bitcast.43), channel_id=1, source_target_pairs={{0,20},{1,21},{2,22},{3,23},{4,16},{5,17},{6,18},{7,19},{8,28},{9,... | collective-permute-start | bytes 4718600 | tf_op jit(solution)/shard_map/ppermute | solution.py:325
  84.6 164.3 %collective-permute-start.3 = (bf16[16,2,64,384]{3,2,1,0:T(8,128)(2,1)S(1)}, bf16[16,2,64,384]{3,2,1,0:T(8,128)(2,1)S(1)}, u32[]{:S(2)}, u32[]{:S(2)}) collective-permute-start(bf16[16,2,64,384]{3,2,1,0:T(8,128)(2,1)S(1)} %bitcast.208), channel_id=1, source_target_pairs={{0,12},{1,13},{2,14},{3,15},{4,8},{5,9},{6,10},{7,11},{8,4},{9,5},... | collective-permute-start | bytes 4718600 | tf_op jit(solution)/shard_map/ppermute | solution.py:325
  131.9 121.7 %collective-permute-start.7 = (bf16[16,2,64,384]{3,2,1,0:T(8,128)(2,1)S(1)}, bf16[16,2,64,384]{3,2,1,0:T(8,128)(2,1)S(1)}, u32[]{:S(2)}, u32[]{:S(2)}) collective-permute-start(bf16[16,2,64,384]{3,2,1,0:T(8,128)(2,1)S(1)} %bitcast.207), channel_id=1, source_target_pairs={{0,24},{1,25},{2,26},{3,27},{4,28},{5,29},{6,30},{7,31},{8,16},{9,... | collective-permute-start | bytes 4718600 | tf_op jit(solution)/shard_map/ppermute | solution.py:325
  199.3 67.7 %collective-permute-start.10 = (bf16[16,2,64,384]{3,2,1,0:T(8,128)(2,1)S(1)}, bf16[16,2,64,384]{3,2,1,0:T(8,128)(2,1)S(1)}, u32[]{:S(2)}, u32[]{:S(2)}) collective-permute-start(bf16[16,2,64,384]{3,2,1,0:T(8,128)(2,1)S(1)} %bitcast.206), channel_id=1, source_target_pairs={{0,28},{1,29},{2,30},{3,31},{4,24},{5,25},{6,26},{7,27},{8,20},{9,... | collective-permute-start | bytes 4718600 | tf_op jit(solution)/shard_map/ppermute | solution.py:325
  204.2 42.2 %collective-permute-start.1 = (bf16[16,2,64,128]{3,2,1,0:T(8,128)(2,1)S(1)}, bf16[16,2,64,128]{3,2,1,0:T(8,128)(2,1)S(1)}, u32[]{:S(2)}, u32[]{:S(2)}) collective-permute-start(bf16[16,2,64,128]{3,2,1,0:T(8,128)(2,1)S(1)} %bitcast.226), channel_id=1, source_target_pairs={{0,4},{1,5},{2,6},{3,7},{4,0},{5,1},{6,2},{7,3},{8,12},{9,13},{10,... | collective-permute-start | bytes 1572872 | tf_op jit(solution)/shard_map/ppermute | solution.py:325
  248.8 118.7 %collective-permute-start.5 = (bf16[16,2,64,128]{3,2,1,0:T(8,128)(2,1)S(1)}, bf16[16,2,64,128]{3,2,1,0:T(8,128)(2,1)}, u32[]{:S(2)}, u32[]{:S(2)}) collective-permute-start(bf16[16,2,64,128]{3,2,1,0:T(8,128)(2,1)S(1)} %bitcast.212), channel_id=1, source_target_pairs={{0,12},{1,13},{2,14},{3,15},{4,8},{5,9},{6,10},{7,11},{8,4},{9,5},... | collective-permute-start | bytes 1572872 | tf_op jit(solution)/shard_map/ppermute | solution.py:325
  250.6 108.1 %collective-permute-start.4 = (bf16[16,2,64,128]{3,2,1,0:T(8,128)(2,1)S(1)}, bf16[16,2,64,128]{3,2,1,0:T(8,128)(2,1)}, u32[]{:S(2)}, u32[]{:S(2)}) collective-permute-start(bf16[16,2,64,128]{3,2,1,0:T(8,128)(2,1)S(1)} %bitcast.214), channel_id=1, source_target_pairs={{0,8},{1,9},{2,10},{3,11},{4,12},{5,13},{6,14},{7,15},{8,0},{9,1},... | collective-permute-start | bytes 1572872 | tf_op jit(solution)/shard_map/ppermute | solution.py:325
  253.6 59.8 %copy-start.5 = (bf16[16,2,64,384]{3,2,1,0:T(8,128)(2,1)}, bf16[16,2,64,384]{3,2,1,0:T(8,128)(2,1)S(1)}, u32[]{:S(2)}) copy-start(bf16[16,2,64,384]{3,2,1,0:T(8,128)(2,1)S(1)} %collective-permute-done.7.refs_6_) | copy-start | bytes 4718596
  255.3 99.3 %collective-permute-start.8 = (bf16[16,2,64,128]{3,2,1,0:T(8,128)(2,1)S(1)}, bf16[16,2,64,128]{3,2,1,0:T(8,128)(2,1)S(1)}, u32[]{:S(2)}, u32[]{:S(2)}) collective-permute-start(bf16[16,2,64,128]{3,2,1,0:T(8,128)(2,1)S(1)} %bitcast.222), channel_id=1, source_target_pairs={{0,16},{1,17},{2,18},{3,19},{4,20},{5,21},{6,22},{7,23},{8,24},{9,... | collective-permute-start | bytes 1572872 | tf_op jit(solution)/shard_map/ppermute | solution.py:325
  268.7 91.3 %collective-permute-start.11 = (bf16[16,2,64,128]{3,2,1,0:T(8,128)(2,1)S(1)}, bf16[16,2,64,128]{3,2,1,0:T(8,128)(2,1)S(1)}, u32[]{:S(2)}, u32[]{:S(2)}) collective-permute-start(bf16[16,2,64,128]{3,2,1,0:T(8,128)(2,1)S(1)} %bitcast.221), channel_id=1, source_target_pairs={{0,20},{1,21},{2,22},{3,23},{4,16},{5,17},{6,18},{7,19},{8,28},{9,... | collective-permute-start | bytes 1572872 | tf_op jit(solution)/shard_map/ppermute | solution.py:325
  357.3 16.9 %collective-permute-start.12 = (bf16[16,2,64,128]{3,2,1,0:T(8,128)(2,1)S(1)}, bf16[16,2,64,128]{3,2,1,0:T(8,128)(2,1)S(1)}, u32[]{:S(2)}, u32[]{:S(2)}) collective-permute-start(bf16[16,2,64,128]{3,2,1,0:T(8,128)(2,1)S(1)} %bitcast.220), channel_id=1, source_target_pairs={{0,24},{1,25},{2,26},{3,27},{4,28},{5,29},{6,30},{7,31},{8,16},{9,... | collective-permute-start | bytes 1572872 | tf_op jit(solution)/shard_map/ppermute | solution.py:325
  361.3 50.2 %collective-permute-start.16 = (bf16[2,64,16,384]{3,2,1,0:T(8,128)(2,1)}, bf16[2,64,16,384]{3,2,1,0:T(8,128)(2,1)S(1)}, u32[]{:S(2)}, u32[]{:S(2)}) collective-permute-start(bf16[2,64,16,384]{3,2,1,0:T(8,128)(2,1)} %dynamic-slice_bitcast_fusion.5), channel_id=1, source_target_pairs={{0,4},{1,5},{2,6},{3,7},{4,0},{5,1},{6,2},{7,3},{8,12},{9,13},{10,... | collective-permute-start | bytes 4718600 | tf_op jit(solution)/shard_map/ppermute | solution.py:325
  364.0 29.9 %collective-permute-start.13 = (bf16[16,2,64,128]{3,2,1,0:T(8,128)(2,1)S(1)}, bf16[16,2,64,128]{3,2,1,0:T(8,128)(2,1)}, u32[]{:S(2)}, u32[]{:S(2)}) collective-permute-start(bf16[16,2,64,128]{3,2,1,0:T(8,128)(2,1)S(1)} %bitcast.223), channel_id=1, source_target_pairs={{0,28},{1,29},{2,30},{3,31},{4,24},{5,25},{6,26},{7,27},{8,20},{9,... | collective-permute-start | bytes 1572872 | tf_op jit(solution)/shard_map/ppermute | solution.py:325
  368.8 69.2 %collective-permute-start.14 = (bf16[2,64,16,384]{3,2,1,0:T(8,128)(2,1)}, bf16[2,64,16,384]{3,2,1,0:T(8,128)(2,1)}, u32[]{:S(2)}, u32[]{:S(2)}) collective-permute-start(bf16[2,64,16,384]{3,2,1,0:T(8,128)(2,1)} %dynamic-slice_bitcast_fusion.6), channel_id=1, source_target_pairs={{0,8},{1,9},{2,10},{3,11},{4,12},{5,13},{6,14},{7,15},{8,0},{9,1},... | collective-permute-start | bytes 4718600 | tf_op jit(solution)/shard_map/ppermute | solution.py:325
  375.5 129.0 %collective-permute-start.20 = (bf16[2,64,16,384]{3,2,1,0:T(8,128)(2,1)}, bf16[2,64,16,384]{3,2,1,0:T(8,128)(2,1)}, u32[]{:S(2)}, u32[]{:S(2)}) collective-permute-start(bf16[2,64,16,384]{3,2,1,0:T(8,128)(2,1)} %dynamic-slice_bitcast_fusion.3), channel_id=1, source_target_pairs={{0,16},{1,17},{2,18},{3,19},{4,20},{5,21},{6,22},{7,23},{8,24},{9,... | collective-permute-start | bytes 4718600 | tf_op jit(solution)/shard_map/ppermute | solution.py:325
  396.6 175.5 %collective-permute-start.23 = (bf16[2,64,16,384]{3,2,1,0:T(8,128)(2,1)}, bf16[2,64,16,384]{3,2,1,0:T(8,128)(2,1)}, u32[]{:S(2)}, u32[]{:S(2)}) collective-permute-start(bf16[2,64,16,384]{3,2,1,0:T(8,128)(2,1)} %dynamic-slice_bitcast_fusion.1), channel_id=1, source_target_pairs={{0,20},{1,21},{2,22},{3,23},{4,16},{5,17},{6,18},{7,19},{8,28},{9,... | collective-permute-start | bytes 4718600 | tf_op jit(solution)/shard_map/ppermute | solution.py:325
  414.2 165.8 %collective-permute-start.17 = (bf16[2,64,16,384]{3,2,1,0:T(8,128)(2,1)}, bf16[2,64,16,384]{3,2,1,0:T(8,128)(2,1)S(1)}, u32[]{:S(2)}, u32[]{:S(2)}) collective-permute-start(bf16[2,64,16,384]{3,2,1,0:T(8,128)(2,1)} %dynamic-slice_bitcast_fusion.4), channel_id=1, source_target_pairs={{0,12},{1,13},{2,14},{3,15},{4,8},{5,9},{6,10},{7,11},{8,4},{9,5},... | collective-permute-start | bytes 4718600 | tf_op jit(solution)/shard_map/ppermute | solution.py:325
  438.0 274.3 %copy-start.1 = (bf16[8,2,16,64,128]{4,2,3,1,0:T(8,128)(2,1)}, bf16[8,2,16,64,128]{4,2,3,1,0:T(8,128)(2,1)S(1)}, u32[]{:S(2)}) copy-start(bf16[8,2,16,64,128]{4,2,3,1,0:T(8,128)(2,1)S(1)} %copy.55) | copy-start | bytes 12582916
  506.1 79.6 %collective-permute-start.21 = (bf16[2,64,16,384]{3,2,1,0:T(8,128)(2,1)S(1)}, bf16[2,64,16,384]{3,2,1,0:T(8,128)(2,1)S(1)}, u32[]{:S(2)}, u32[]{:S(2)}) collective-permute-start(bf16[2,64,16,384]{3,2,1,0:T(8,128)(2,1)S(1)} %dynamic-slice_bitcast_fusion.2), channel_id=1, source_target_pairs={{0,24},{1,25},{2,26},{3,27},{4,28},{5,29},{6,30},{7,31},{8,16},{9,... | collective-permute-start | bytes 4718600 | tf_op jit(solution)/shard_map/ppermute | solution.py:325
  507.6 69.3 %collective-permute-start.15 = (bf16[2,64,16,128]{3,2,1,0:T(8,128)(2,1)S(1)}, bf16[2,64,16,128]{3,2,1,0:T(8,128)(2,1)S(1)}, u32[]{:S(2)}, u32[]{:S(2)}) collective-permute-start(bf16[2,64,16,128]{3,2,1,0:T(8,128)(2,1)S(1)} %dynamic-slice_bitcast_fusion.29), channel_id=1, source_target_pairs={{0,4},{1,5},{2,6},{3,7},{4,0},{5,1},{6,2},{7,3},{8,12},{9,13},{10,... | collective-permute-start | bytes 1572872 | tf_op jit(solution)/shard_map/ppermute | solution.py:325
  573.6 73.6 %collective-permute-start.24 = (bf16[2,64,16,384]{3,2,1,0:T(8,128)(2,1)S(1)}, bf16[2,64,16,384]{3,2,1,0:T(8,128)(2,1)S(1)}, u32[]{:S(2)}, u32[]{:S(2)}) collective-permute-start(bf16[2,64,16,384]{3,2,1,0:T(8,128)(2,1)S(1)} %dynamic-slice_bitcast_fusion), channel_id=1, source_target_pairs={{0,28},{1,29},{2,30},{3,31},{4,24},{5,25},{6,26},{7,27},{8,20},{9,... | collective-permute-start | bytes 4718600 | tf_op jit(solution)/shard_map/ppermute | solution.py:325
  577.0 180.5 %collective-permute-start.19 = (bf16[2,64,16,128]{3,2,1,0:T(8,128)(2,1)S(1)}, bf16[2,64,16,128]{3,2,1,0:T(8,128)(2,1)S(1)}, u32[]{:S(2)}, u32[]{:S(2)}) collective-permute-start(bf16[2,64,16,128]{3,2,1,0:T(8,128)(2,1)S(1)} %dynamic-slice_bitcast_fusion.27), channel_id=1, source_target_pairs={{0,12},{1,13},{2,14},{3,15},{4,8},{5,9},{6,10},{7,11},{8,4},{9,5},... | collective-permute-start | bytes 1572872 | tf_op jit(solution)/shard_map/ppermute | solution.py:325
  580.8 175.9 %collective-permute-start.18 = (bf16[2,64,16,128]{3,2,1,0:T(8,128)(2,1)}, bf16[2,64,16,128]{3,2,1,0:T(8,128)(2,1)S(1)}, u32[]{:S(2)}, u32[]{:S(2)}) collective-permute-start(bf16[2,64,16,128]{3,2,1,0:T(8,128)(2,1)} %dynamic-slice_bitcast_fusion.28), channel_id=1, source_target_pairs={{0,8},{1,9},{2,10},{3,11},{4,12},{5,13},{6,14},{7,15},{8,0},{9,1},... | collective-permute-start | bytes 1572872 | tf_op jit(solution)/shard_map/ppermute | solution.py:325
  585.8 126.5 %collective-permute-start.22 = (bf16[2,64,16,128]{3,2,1,0:T(8,128)(2,1)S(1)}, bf16[2,64,16,128]{3,2,1,0:T(8,128)(2,1)S(1)}, u32[]{:S(2)}, u32[]{:S(2)}) collective-permute-start(bf16[2,64,16,128]{3,2,1,0:T(8,128)(2,1)S(1)} %dynamic-slice_bitcast_fusion.26), channel_id=1, source_target_pairs={{0,16},{1,17},{2,18},{3,19},{4,20},{5,21},{6,22},{7,23},{8,24},{9,... | collective-permute-start | bytes 1572872 | tf_op jit(solution)/shard_map/ppermute | solution.py:325
  648.1 104.9 %collective-permute-start.25 = (bf16[2,64,16,128]{3,2,1,0:T(8,128)(2,1)}, bf16[2,64,16,128]{3,2,1,0:T(8,128)(2,1)S(1)}, u32[]{:S(2)}, u32[]{:S(2)}) collective-permute-start(bf16[2,64,16,128]{3,2,1,0:T(8,128)(2,1)} %dynamic-slice_bitcast_fusion.25), channel_id=1, source_target_pairs={{0,20},{1,21},{2,22},{3,23},{4,16},{5,17},{6,18},{7,19},{8,28},{9,... | collective-permute-start | bytes 1572872 | tf_op jit(solution)/shard_map/ppermute | solution.py:325
  713.2 46.8 %collective-permute-start.26 = (bf16[2,64,16,128]{3,2,1,0:T(8,128)(2,1)}, bf16[2,64,16,128]{3,2,1,0:T(8,128)(2,1)S(1)}, u32[]{:S(2)}, u32[]{:S(2)}) collective-permute-start(bf16[2,64,16,128]{3,2,1,0:T(8,128)(2,1)} %dynamic-slice_bitcast_fusion.24), channel_id=1, source_target_pairs={{0,24},{1,25},{2,26},{3,27},{4,28},{5,29},{6,30},{7,31},{8,16},{9,... | collective-permute-start | bytes 1572872 | tf_op jit(solution)/shard_map/ppermute | solution.py:325
  754.0 12.0 %collective-permute-start.27 = (bf16[2,64,16,128]{3,2,1,0:T(8,128)(2,1)S(1)}, bf16[2,64,16,128]{3,2,1,0:T(8,128)(2,1)S(1)}, u32[]{:S(2)}, u32[]{:S(2)}) collective-permute-start(bf16[2,64,16,128]{3,2,1,0:T(8,128)(2,1)S(1)} %dynamic-slice_bitcast_fusion.23), channel_id=1, source_target_pairs={{0,28},{1,29},{2,30},{3,31},{4,24},{5,25},{6,26},{7,27},{8,20},{9,... | collective-permute-start | bytes 1572872 | tf_op jit(solution)/shard_map/ppermute | solution.py:325
  (9 other events, 215.7 us)
Sparse Core Ops, SparseCore 0:
  8.9 204.2 all-gather.2
  214.8 201.5 all-gather.4

commit v4 on v3

--- a/solution.py
+++ b/solution.py
@@ -18,6 +18,7 @@
 
 FAR_WINDOW = 2
 NEAR_WINDOW = 2
+LATE_WINDOW = 5
 VMEM_BYTES = 56 * 1024 * 1024
 
 
@@ -66,12 +67,12 @@
     weight = -weight_ref[0]
     less = jnp.dot(
         table,
-        jnp.concatenate([ref[0, 0] for ref in x_refs], axis=0),
+        jnp.concatenate([ref[0, 0, 0] for ref in x_refs], axis=0),
         preferred_element_type=jnp.float32,
     )
     more = jnp.dot(
         table,
-        jnp.concatenate([ref[0, 1] for ref in x_refs], axis=0),
+        jnp.concatenate([ref[0, 0, 1] for ref in x_refs], axis=0),
         preferred_element_type=jnp.float32,
     )
     less_re, less_im = (less[:half], less[half:])
@@ -107,14 +108,22 @@
 
 
 def born(order, spread, forward, backward, weight, mask):
+    if isinstance(spread, list):
+        places = [lambda i, order: (0, i, 0, 0, 0)] * len(spread)
+    else:
+        places = [
+            lambda i, order, place=place: (order[place], i, 0, 0, 0)
+            for place in range(spread.shape[0])
+        ]
+        spread = [spread] * len(places)
     pieces = len(spread)
-    sub_rows, _, depth, width = spread[0].shape
+    _, sub_rows, _, depth, width = spread[0].shape
     size = pieces * depth
     out_shape = (pieces, 2, sub_rows, depth, width)
     grid_spec = pltpu.PrefetchScalarGridSpec(
         num_scalar_prefetch=1,
         grid=(sub_rows,),
-        in_specs=[pl.BlockSpec((1, 2, depth, width), lambda i, order: (i, 0, 0, 0))] * pieces
+        in_specs=[pl.BlockSpec((1, 1, 2, depth, width), place) for place in places]
         + [
             pl.BlockSpec((size, size), lambda i, order: (0, 0)),
             pl.BlockSpec((size, size), lambda i, order: (0, 0)),
@@ -148,9 +157,9 @@
     return value.reshape(value.shape[0] * value.shape[1], value.shape[2])
 
 
-def complex_left(terms, index, order_ref):
-    re = [sigma_rows(ref, kind, 0, index, order_ref) for ref, kind in terms]
-    im = [sigma_rows(ref, kind, 1, index, order_ref) for ref, kind in terms]
+def complex_left(terms, index):
+    re = [sigma_rows(ref, kind, 0, index, order_ref) for ref, order_ref, kind in terms]
+    im = [sigma_rows(ref, kind, 1, index, order_ref) for ref, order_ref, kind in terms]
     top, low = (re + [-v for v in im], im + re)
     return jnp.concatenate(
         [jnp.concatenate(top, axis=1), jnp.concatenate(low, axis=1)], axis=0
@@ -159,9 +168,8 @@
 
 def collide_kernel(plan, order_ref, *refs):
     count, ret_terms, less_terms, first_col, gap_step, gap_col, has_total, has_old, has_rest, mixed = plan
-    order_ref = order_ref if mixed else None
     refs = list(refs)
-    sources = [refs.pop(0) for _ in range(count)]
+    sources = [(refs.pop(0), order_ref if place in mixed else None) for place in range(count)]
     lesser_ref = refs.pop(0) if ret_terms else None
     gap_less_ref, gap_more_ref = (refs.pop(0), refs.pop(0))
     total_ref = refs.pop(0) if has_total else None
@@ -170,13 +178,13 @@
     out_ref = refs.pop(0) if not has_rest or len(refs) == 2 else None
     rest_ref = refs.pop(0) if has_rest else None
     block, steps, gap_cols = gap_less_ref.shape[1:]
-    rows = sources[0].shape[0] * sources[0].shape[4]
+    rows = sources[0][0].shape[0] * sources[0][0].shape[4]
     done_cols = out_ref.shape[3] if out_ref is not None else 0
     shape = (steps, gap_cols)
     step_index = gap_step + lax.broadcasted_iota(jnp.int32, shape, 0)
     upper = step_index <= gap_col + lax.broadcasted_iota(jnp.int32, shape, 1)
-    ret_terms = [(sources[source], kind) for source, kind in ret_terms]
-    less_terms = [(sources[source], kind) for source, kind in less_terms]
+    ret_terms = [(*sources[source], kind) for source, kind in ret_terms]
+    less_terms = [(*sources[source], kind) for source, kind in less_terms]
     for index in range(block):
 
         def advanced(part):
@@ -189,12 +197,12 @@
                 left, jnp.concatenate(right, axis=0), preferred_element_type=jnp.float32
             )
 
-        left = complex_left(less_terms, index, order_ref)
+        left = complex_left(less_terms, index)
         if not ret_terms:
             value = product(left, advanced(0), advanced(1))
         elif gap_col == first_col:
             value = product(
-                jnp.concatenate([left, complex_left(ret_terms, index, order_ref)], axis=1),
+                jnp.concatenate([left, complex_left(ret_terms, index)], axis=1),
                 advanced(0),
                 advanced(1),
                 lesser_ref[0, index],
@@ -202,7 +210,7 @@
             )
         else:
             value = product(
-                complex_left(ret_terms, index, order_ref), lesser_ref[0, index], lesser_ref[1, index]
+                complex_left(ret_terms, index), lesser_ref[0, index], lesser_ref[1, index]
             )
             skipped = gap_col - first_col
             value = jnp.concatenate(
@@ -222,7 +230,7 @@
                 rest_ref[part, index] = one[:, done_cols:]
 
 
-def collide(order, sources, ret, less, functions, carried, cols, block, mixed=False):
+def collide(order, sources, ret, less, functions, carried, cols, block, mixed=()):
     ret_terms, ret_step, ret_steps = ret
     less_terms, gap_step, gap_steps, gap_col = less
     less_all, more_all = functions
@@ -314,14 +322,17 @@
     order = group ^ jnp.arange(groups, dtype=jnp.int32)
     far, near = (list(range(groups // 2, groups)), list(range(1, groups // 2)))
     offsets = [d for pair in zip(far, near + [0]) for d in pair if d]
-    arrived = {True: [], False: []}
-
-    def send(make, arrays, offset):
-        is_far = 2 * offset >= groups
-        queue, ahead = (arrived[is_far], FAR_WINDOW if is_far else NEAR_WINDOW)
+    queues = {"far": (FAR_WINDOW, []), "near": (NEAR_WINDOW, []), "late": (LATE_WINDOW, [])}
+    everyone = list(range(ranks))
+    width = col_count // 4
+    late_ranks = [r for r in everyone if (r + 1) * row_count > 3 * width]
+
+    def send(make, arrays, offset, on_ranks):
+        name = "far" if 2 * offset >= groups else "near"
+        ahead, queue = queues["late" if on_ranks != everyone else name]
         if len(queue) >= ahead:
             arrays, _ = lax.optimization_barrier((arrays, queue[-ahead]))
-        pairs = [(g * ranks + r, (g ^ offset) * ranks + r) for g in range(groups) for r in range(ranks)]
+        pairs = [(g * ranks + r, (g ^ offset) * ranks + r) for g in range(groups) for r in on_ranks]
         queue.append(lax.ppermute(make(*arrays), ("mom", "trow"), pairs))
         return queue[-1]
 
@@ -334,20 +345,26 @@
             )
 
         both = jnp.stack([rows_of(array) for array in arrays])
-        return both.transpose(3, 0, 1, 2, 4).reshape(sub_rows, 2, depth, count)
-
-    width = col_count // 4
+        return both.transpose(3, 0, 1, 2, 4).reshape(1, sub_rows, 2, depth, count)
+
+    def swap(array):
+        return lax.all_to_all(array, "mom", split_axis=0, concat_axis=0, tiled=True)
+
     halves = [(0, 3 * width), (3 * width, width)]
     row_first = lax.axis_index("trow") * row_count + group * sub_rows
     row_times = row_first + jnp.arange(sub_rows, dtype=jnp.int32)
-    spreads = []
-    for first, count in halves:
-        spread = {0: pack(0, first, count, (lesser, greater))}
-        for d in offsets:
-            spread[d] = send(
-                lambda *arrays: pack(d, first, count, arrays), (lesser, greater), d
-            )
-        spreads.append([spread[d] for d in range(groups)])
+    first, count = halves[0]
+    spread = {0: pack(0, first, count, (lesser, greater))}
+    for d in offsets:
+        spread[d] = send(
+            lambda *arrays: pack(d, first, count, arrays), (lesser, greater), d, everyone
+        )
+    first, count = halves[1]
+    both = jnp.stack([lesser[..., first:], greater[..., first:]])
+    both = both.reshape(2, 2, local_k, groups, sub_rows, count).transpose(3, 4, 0, 1, 2, 5)
+    both, _ = lax.optimization_barrier((both, [spread[d] for d in offsets]))
+    both = swap(both.reshape(groups, sub_rows, 2, depth, count))
+    spreads = [[spread[d] for d in range(groups)], both]
 
     functions = tuple(
         lax.all_gather(array, "trow", axis=2, tiled=True) for array in (lesser, greater)
@@ -367,51 +384,48 @@
         sigma = born(order, spreads[part], forward, backward, weight[:, None], mask[:, None])
         return with_layout_constraint(sigma.transpose(0, 1, 3, 2, 4), Layout((0, 1, 2, 3, 4)))
 
-    def exchange(make, sigma, before=None, before_last=None):
-        got = {}
-        for d in offsets:
-            after = before_last if d == far[-1] and before_last is not None else before
-            held = sigma
-            if after is not None:
-                held, _ = lax.optimization_barrier((sigma, after))
-            got[d] = send(lambda array: make(array[group ^ d]), (held,), d)
-        got[0] = make(sigma[group])
-        got = jnp.stack([got[d] for d in range(groups)])
+    def late_ret(sigma):
+        got = {0: sigma[group][1:]}
+        for d in [*far, *near]:
+            got[d] = send(lambda array: array[group ^ d][1:], (sigma,), d, late_ranks)
+        return in_order(jnp.stack([got[d] for d in range(groups)]), True)
+
+    def in_order(got, mixed):
         kinds, count = (got.shape[1], got.shape[4])
         got = got.reshape(groups, kinds, 2, local_k, sub_rows, count)
         if sub_rows % 16 == 0:
             return got
-        got = got[order].transpose(1, 2, 3, 0, 4, 5)
+        got = (got[order] if mixed else got).transpose(1, 2, 3, 0, 4, 5)
         return got.reshape(1, kinds, 2, local_k, groups * sub_rows, count)
 
-    mixed = sub_rows % 16 == 0
-    sigma = born_part(0)
-    low = exchange(lambda array: array, sigma)
-    low_total, _ = collide(
+    sigma, _ = lax.optimization_barrier((born_part(0), spreads[1]))
+    low = in_order(swap(sigma), False)
+    sigma = born_part(1)
+    high_ret = late_ret(sigma)
+    high, _ = lax.optimization_barrier((sigma[:, :1], (low, high_ret)))
+    high = in_order(swap(high), False)
+    carried = collide(
         order,
-        [low],
-        ([(0, 1)], 0, 3 * width),
+        [low, high_ret],
+        ([(0, 1), (1, 0)], 0, col_count),
         ([(0, 0)], 0, 3 * width, 0),
         functions,
         (None, None),
-        (0, 0),
+        (0, 3 * width),
         2,
-        mixed,
-    )
-    sigma = born_part(1)
-    high = exchange(lambda array: array, sigma, None, low_total)
-    _, output = collide(
+        () if sub_rows % 16 else (1,),
+    )
+    carried = collide(
         order,
         [high],
-        ([(0, 1)], 3 * width, width),
+        ((), 0, 0),
         ([(0, 0)], 3 * width, width, 3 * width),
         functions,
-        (low_total, None),
-        (0, col_count),
-        4,
-        mixed,
-    )
-    return output
+        carried,
+        (3 * width, col_count),
+        8,
+    )
+    return carried[1]
 
 
 def solution(mesh):

time: 793 us -> 777 us (0.980)
  the two profiles are of different devices: /device:TPU:0 before, /device:TPU:7 now
where the time goes in v4:
time: 777 us; the launch traced here: 775 us
  waiting for transfers between devices  496 us (64%)
  Pallas kernels  94.3 us (12%)
  starting transfers between devices  90.7 us (12%)
  local copies, waits for them, and re-layouts  68.6 us (9%)
  between operations  14.5 us (2%)
  other arithmetic  10.2 us (1%)
    ppermute x14, waiting for transfers between devices, send(): queue.append(lax.ppermute(make(*arrays), ('mom', 'trow'), pairs))  458 us
    all_to_all x3, starting transfers between devices, swap(): return lax.all_to_all(array, 'mom', split_axis=0, concat_axis=0, tiled=True)  53.8 us
    pallas_call x2, Pallas kernels, born(): pl.pallas_call(functools.partial(born_kernel, pieces), grid_spec=grid_spe...  47.8 us
    pallas_call x2, Pallas kernels, collide(): pl.pallas_call(functools.partial(collide_kernel, plan), grid_spec=pltpu.P...  46.5 us
    all_to_all x3, waiting for transfers between devices, swap(): return lax.all_to_all(array, 'mom', split_axis=0, concat_axis=0, tiled=True)  37.3 us
    ppermute x14, starting transfers between devices, send(): queue.append(lax.ppermute(make(*arrays), ('mom', 'trow'), pairs))  36.9 us
    pallas_call x2, local copies, waits for them, and re-layouts, born(): pl.pallas_call(functools.partial(born_kernel, pieces), grid_spec=grid_spe...  21.2 us
  transfers between devices with their start and end apart: 19, of which 6 were waited for; matrix products, arithmetic and copies ran while one was open for 9% of the time, Pallas kernels for 11%

profile of v4, /device:TPU:7, one launch (start us, length us, event | category | flops | bytes accessed | tf_op | source)
XLA Modules:
  0.0 774.6 jit_solution(1480700908092522788)
XLA Ops:
  8.0 2.5 dynamic-slice_bitcast_fusion
  10.6 2.5 dynamic-slice_bitcast_fusion.1
  15.1 2.3 collective-permute-start
  23.9 95.1 %collective-permute-done.refs_4_ = bf16[1,16,2,64,384]{4,3,2,1,0:T(8,128)(2,1)} collective-permute-done((bf16[1,16,2,64,384]{4,3,2,1,0:T(8,128)(2,1)}, bf16[1,16,2,64,384]{4,3,2,1,0:T(8,128)(2,1)}, u32[]{:S(2)}, u32[]{:S(2)}) %collective-permute-start) | collective-permute-done | bytes 1572896 | tf_op jit(solution)/shard_map/ppermute | solution.py:336
  122.1 4.2 collective-permute-start.4
  129.5 56.9 %collective-permute-done.2.refs_5_ = bf16[1,16,2,64,384]{4,3,2,1,0:T(8,128)(2,1)} collective-permute-done((bf16[1,16,2,64,384]{4,3,2,1,0:T(8,128)(2,1)}, bf16[1,16,2,64,384]{4,3,2,1,0:T(8,128)(2,1)}, u32[]{:S(2)}, u32[]{:S(2)}) %collective-permute-start.2) | collective-permute-done | bytes 1572896 | tf_op jit(solution)/shard_map/ppermute | solution.py:336
  189.5 5.2 collective-permute-start.6
  194.7 1.7 slice.56
  196.4 1.7 slice.55
  200.9 2.4 maximum_bitcast_fusion
  203.3 51.4 %collective-permute-done.5.refs_3_ = bf16[1,16,2,64,384]{4,3,2,1,0:T(8,128)(2,1)S(1)} collective-permute-done((bf16[1,16,2,64,384]{4,3,2,1,0:T(8,128)(2,1)S(1)}, bf16[1,16,2,64,384]{4,3,2,1,0:T(8,128)(2,1)S(1)}, u32[]{:S(2)}, u32[]{:S(2)}) %collective-permute-start.5) | collective-permute-done | bytes 1572896 | tf_op jit(solution)/shard_map/ppermute | solution.py:336
  257.0 37.5 %all-to-all-start = ((bf16[8,16,2,64,128]{4,3,2,1,0:T(8,128)(2,1)}), bf16[8,16,2,64,128]{4,3,2,1,0:T(8,128)(2,1)}, u32[]{:S(2)}, u32[]{:S(2)}) async-start(bf16[8,16,2,64,128]{4,3,2,1,0:T(8,128)(2,1)} %bitcast.111), calls=%async_computation | async-start | bytes 8388608 | tf_op jit(solution)/shard_map/all_to_all | solution.py:351
  305.8 28.6 %born.3 = bf16[8,2,16,64,384]{4,3,2,1,0:T(8,128)(2,1)} custom-call(s32[8]{0:T(128)} %iota_xor_fusion.order_ref, bf16[1,16,2,64,384]{4,3,2,1,0:T(8,128)(2,1)} %bitcast.128, bf16[1,16,2,64,384]{4,3,2,1,0:T(8,128)(2,1)} %collective-permute-done.1.refs_1_, bf16[1,16,2,64,384]{4,3,2,1,0:T(8,128)(2,1)} %collective-permute-done.3.refs_2_, ...), custom_call_target="tpu_custom_call" | custom-call | flops 12884901888 | bytes 25165824 | tf_op jit(solution)/shard_map/born/pallas_call | solution.py:137
  334.4 15.5 %copy.45 = bf16[8,2,16,64,384]{4,2,3,1,0:T(8,128)(2,1)} copy(bf16[8,2,16,64,384]{4,3,2,1,0:T(8,128)(2,1)} %born.3) | data formatting | bytes 25165824 | tf_op jit(solution)/shard_map/born/pallas_call | solution.py:137
  349.9 37.3 %all-to-all-done.refs_0_.refs_1_.refs_2_.refs_3_.refs_4_.refs_5_.refs_6_.refs_7_ = bf16[8,16,2,64,128]{4,3,2,1,0:T(8,128)(2,1)} async-done(((bf16[8,16,2,64,128]{4,3,2,1,0:T(8,128)(2,1)}), bf16[8,16,2,64,128]{4,3,2,1,0:T(8,128)(2,1)}, u32[]{:S(2)}, u32[]{:S(2)}) %all-to-all-start) | async-done | bytes 4194336 | tf_op jit(solution)/shard_map/all_to_all | solution.py:351
  387.2 7.0 all-to-all-start.1
  395.6 19.3 %born.2 = bf16[8,2,16,64,128]{4,3,2,1,0:T(8,128)(2,1)} custom-call(s32[8]{0:T(128)} %iota_xor_fusion.order_ref, bf16[8,16,2,64,128]{4,3,2,1,0:T(8,128)(2,1)} %all-to-all-done.refs_0_.refs_1_.refs_2_.refs_3_.refs_4_.refs_5_.refs_6_.refs_7_, bf16[8,16,2,64,128]{4,3,2,1,0:T(8,128)(2,1)} %all-to-all-done.refs_0_.refs_1_.refs_2_.refs_3_.refs_4_.refs_5_.refs_6_.refs_7_, ...), custom_call_target="tpu_custom_call" | custom-call | flops 4294967296 | bytes 8388608 | tf_op jit(solution)/shard_map/born/pallas_call | solution.py:137
  414.9 5.7 copy.46
  420.6 2.0 copy-done
  422.9 4.0 collective-permute-start.8
  426.9 2.3 collective-permute-start.10
  429.2 3.0 collective-permute-start.7
  432.2 243.4 %collective-permute-done.8 = bf16[1,64,16,128]{3,2,1,0:T(8,128)(2,1)S(1)} collective-permute-done((bf16[1,64,16,128]{3,2,1,0:T(8,128)(2,1)S(1)}, bf16[1,64,16,128]{3,2,1,0:T(8,128)(2,1)S(1)}, u32[]{:S(2)}, u32[]{:S(2)}) %collective-permute-start.8) | collective-permute-done | bytes 262176 | tf_op jit(solution)/shard_map/ppermute | solution.py:336
  676.6 1.9 collective-permute-start.9
  679.5 3.4 collective-permute-start.11
  683.6 3.3 slice.75
  686.9 3.9 collective-permute-start.12
  690.8 4.1 collective-permute-start.13
  696.3 10.6 %collective-permute-done.11 = bf16[1,64,16,128]{3,2,1,0:T(8,128)(2,1)S(1)} collective-permute-done((bf16[1,64,16,128]{3,2,1,0:T(8,128)(2,1)S(1)}, bf16[1,64,16,128]{3,2,1,0:T(8,128)(2,1)S(1)}, u32[]{:S(2)}, u32[]{:S(2)}) %collective-permute-start.11) | collective-permute-done | bytes 262176 | tf_op jit(solution)/shard_map/ppermute | solution.py:336
  710.6 9.3 %all-to-all-start.2 = ((bf16[8,1,64,16,128]{4,3,2,1,0:T(8,128)(2,1)}), bf16[8,1,64,16,128]{4,3,2,1,0:T(8,128)(2,1)S(1)}, u32[]{:S(2)}, u32[]{:S(2)}) async-start(bf16[8,1,64,16,128]{4,3,2,1,0:T(8,128)(2,1)} %slice.75), calls=%async_computation.2 | async-start | bytes 4194304 | tf_op jit(solution)/shard_map/all_to_all | solution.py:351
  719.9 39.3 %collide.2 = (bf16[2,32,128,512]{3,2,1,0:T(8,128)(2,1)}, f32[2,32,128,128]{3,2,1,0:T(8,128)}) custom-call(s32[8]{0:T(128)} %iota_xor_fusion.order_ref, bf16[8,2,2,32,16,384]{5,4,3,2,1,0:T(8,128)(2,1)} %bitcast.43.refs_0_, bf16[8,1,2,32,16,128]{5,4,3,2,1,0:T(8,128)(2,1)} %constant_dynamic-update-slice_fusion.refs_1_, ...), custom_call_target="tpu_custom_call" | custom-call | flops 15032385536 | bytes 192937984 | tf_op jit(solution)/shard_map/collide/pallas_call | solution.py:296
  760.5 7.2 collide.3
  (91 shorter events, 45.5 us)
Async XLA Ops:
  6.5 713.3 %all-gather.3.cloned.1.call-start = ((), (), s32[]{:S(2)}) async-start(), calls=%async_computation.3 | async-start | bytes 41943040 | tf_op jit(solution)/shard_map/all_gather | solution.py:370
  7.3 712.6 %all-gather.5.cloned.1.call-start = ((), (), s32[]{:S(2)}) async-start(), calls=%async_computation.4 | async-start | bytes 41943040 | tf_op jit(solution)/shard_map/all_gather | solution.py:370
  15.1 103.9 %collective-permute-start = (bf16[1,16,2,64,384]{4,3,2,1,0:T(8,128)(2,1)}, bf16[1,16,2,64,384]{4,3,2,1,0:T(8,128)(2,1)}, u32[]{:S(2)}, u32[]{:S(2)}) collective-permute-start(bf16[1,16,2,64,384]{4,3,2,1,0:T(8,128)(2,1)} %bitcast.6), channel_id=1, source_target_pairs={{0,16},{1,17},{2,18},{3,19},{4,20},{5,21},{6,22},{7,23},{8,24},{9,... | collective-permute-start | bytes 4718600 | tf_op jit(solution)/shard_map/ppermute | solution.py:336
  18.9 107.4 %collective-permute-start.1 = (bf16[1,16,2,64,384]{4,3,2,1,0:T(8,128)(2,1)}, bf16[1,16,2,64,384]{4,3,2,1,0:T(8,128)(2,1)}, u32[]{:S(2)}, u32[]{:S(2)}) collective-permute-start(bf16[1,16,2,64,384]{4,3,2,1,0:T(8,128)(2,1)} %bitcast.10), channel_id=1, source_target_pairs={{0,4},{1,5},{2,6},{3,7},{4,0},{5,1},{6,2},{7,3},{8,12},{9,13},{10,... | collective-permute-start | bytes 4718600 | tf_op jit(solution)/shard_map/ppermute | solution.py:336
  21.1 165.3 %collective-permute-start.2 = (bf16[1,16,2,64,384]{4,3,2,1,0:T(8,128)(2,1)}, bf16[1,16,2,64,384]{4,3,2,1,0:T(8,128)(2,1)}, u32[]{:S(2)}, u32[]{:S(2)}) collective-permute-start(bf16[1,16,2,64,384]{4,3,2,1,0:T(8,128)(2,1)} %bitcast.14), channel_id=1, source_target_pairs={{0,20},{1,21},{2,22},{3,23},{4,16},{5,17},{6,18},{7,19},{8,28},{9,... | collective-permute-start | bytes 4718600 | tf_op jit(solution)/shard_map/ppermute | solution.py:336
  22.5 180.8 %collective-permute-start.3 = (bf16[1,16,2,64,384]{4,3,2,1,0:T(8,128)(2,1)S(1)}, bf16[1,16,2,64,384]{4,3,2,1,0:T(8,128)(2,1)}, u32[]{:S(2)}, u32[]{:S(2)}) collective-permute-start(bf16[1,16,2,64,384]{4,3,2,1,0:T(8,128)(2,1)S(1)} %bitcast.124), channel_id=1, source_target_pairs={{0,8},{1,9},{2,10},{3,11},{4,12},{5,13},{6,14},{7,15},{8,0},{9,1},... | collective-permute-start | bytes 4718600 | tf_op jit(solution)/shard_map/ppermute | solution.py:336
  122.1 81.2 %collective-permute-start.4 = (bf16[1,16,2,64,384]{4,3,2,1,0:T(8,128)(2,1)S(1)}, bf16[1,16,2,64,384]{4,3,2,1,0:T(8,128)(2,1)S(1)}, u32[]{:S(2)}, u32[]{:S(2)}) collective-permute-start(bf16[1,16,2,64,384]{4,3,2,1,0:T(8,128)(2,1)S(1)} %bitcast.125), channel_id=1, source_target_pairs={{0,24},{1,25},{2,26},{3,27},{4,28},{5,29},{6,30},{7,31},{8,16},{9,... | collective-permute-start | bytes 4718600 | tf_op jit(solution)/shard_map/ppermute | solution.py:336
  129.4 125.3 %collective-permute-start.5 = (bf16[1,16,2,64,384]{4,3,2,1,0:T(8,128)(2,1)S(1)}, bf16[1,16,2,64,384]{4,3,2,1,0:T(8,128)(2,1)S(1)}, u32[]{:S(2)}, u32[]{:S(2)}) collective-permute-start(bf16[1,16,2,64,384]{4,3,2,1,0:T(8,128)(2,1)S(1)} %bitcast.126), channel_id=1, source_target_pairs={{0,12},{1,13},{2,14},{3,15},{4,8},{5,9},{6,10},{7,11},{8,4},{9,5},... | collective-permute-start | bytes 4718600 | tf_op jit(solution)/shard_map/ppermute | solution.py:336
  189.5 65.2 %collective-permute-start.6 = (bf16[1,16,2,64,384]{4,3,2,1,0:T(8,128)(2,1)S(1)}, bf16[1,16,2,64,384]{4,3,2,1,0:T(8,128)(2,1)S(1)}, u32[]{:S(2)}, u32[]{:S(2)}) collective-permute-start(bf16[1,16,2,64,384]{4,3,2,1,0:T(8,128)(2,1)S(1)} %bitcast.127), channel_id=1, source_target_pairs={{0,28},{1,29},{2,30},{3,31},{4,24},{5,25},{6,26},{7,27},{8,20},{9,... | collective-permute-start | bytes 4718600 | tf_op jit(solution)/shard_map/ppermute | solution.py:336
  203.3 51.4 %copy-start.3 = (bf16[1,16,2,64,384]{4,3,2,1,0:T(8,128)(2,1)}, bf16[1,16,2,64,384]{4,3,2,1,0:T(8,128)(2,1)S(1)}, u32[]{:S(2)}) copy-start(bf16[1,16,2,64,384]{4,3,2,1,0:T(8,128)(2,1)S(1)} %collective-permute-done.4.refs_6_) | copy-start | bytes 4718596
  254.7 1.2 copy-start.4
  255.9 1.1 copy-start.5
  257.0 37.5 %copy-start.2 = (s32[256]{0:T(256)S(1)}, s32[256]{0:T(256)}, u32[]{:S(2)}) copy-start(s32[256]{0:T(256)} %param.6) | copy-start | bytes 3076
  257.0 130.2 %all-to-all-start = ((bf16[8,16,2,64,128]{4,3,2,1,0:T(8,128)(2,1)}), bf16[8,16,2,64,128]{4,3,2,1,0:T(8,128)(2,1)}, u32[]{:S(2)}, u32[]{:S(2)}) async-start(bf16[8,16,2,64,128]{4,3,2,1,0:T(8,128)(2,1)} %bitcast.111), calls=%async_computation | async-start | bytes 8388608 | tf_op jit(solution)/shard_map/all_to_all | solution.py:351
  387.2 323.4 %all-to-all-start.1 = ((bf16[8,2,64,16,384]{4,3,2,1,0:T(8,128)(2,1)}), bf16[8,2,64,16,384]{4,3,2,1,0:T(8,128)(2,1)}, u32[]{:S(2)}, u32[]{:S(2)}) async-start(bf16[8,2,64,16,384]{4,3,2,1,0:T(8,128)(2,1)} %bitcast.110), calls=%async_computation.1 | async-start | bytes 25165824 | tf_op jit(solution)/shard_map/all_to_all | solution.py:351
  420.6 2.0 copy-start
  422.9 252.7 %collective-permute-start.8 = (bf16[1,64,16,128]{3,2,1,0:T(8,128)(2,1)S(1)}, bf16[1,64,16,128]{3,2,1,0:T(8,128)(2,1)S(1)}, u32[]{:S(2)}, u32[]{:S(2)}) collective-permute-start(bf16[1,64,16,128]{3,2,1,0:T(8,128)(2,1)S(1)} %get-tuple-element.44), channel_id=1, source_target_pairs={{3,19},{7,23},{11,27},{15,31},{19,3},{23,7},{27,11},{31,15}} | collective-permute-start | bytes 786440 | tf_op jit(solution)/shard_map/ppermute | solution.py:336
  426.9 251.6 %collective-permute-start.10 = (bf16[1,64,16,128]{3,2,1,0:T(8,128)(2,1)S(1)}, bf16[1,64,16,128]{3,2,1,0:T(8,128)(2,1)S(1)}, u32[]{:S(2)}, u32[]{:S(2)}) collective-permute-start(bf16[1,64,16,128]{3,2,1,0:T(8,128)(2,1)S(1)} %get-tuple-element.43), channel_id=1, source_target_pairs={{3,23},{7,19},{11,31},{15,27},{19,7},{23,3},{27,15},{31,11}} | collective-permute-start | bytes 786440 | tf_op jit(solution)/shard_map/ppermute | solution.py:336
  429.2 265.6 %collective-permute-start.7 = (bf16[1,64,16,128]{3,2,1,0:T(8,128)(2,1)S(1)}, bf16[1,64,16,128]{3,2,1,0:T(8,128)(2,1)S(1)}, u32[]{:S(2)}, u32[]{:S(2)}) collective-permute-start(bf16[1,64,16,128]{3,2,1,0:T(8,128)(2,1)S(1)} %get-tuple-element.45), channel_id=1, source_target_pairs={{3,7},{7,3},{11,15},{15,11},{19,23},{23,19},{27,31},{31,27}} | collective-permute-start | bytes 786440 | tf_op jit(solution)/shard_map/ppermute | solution.py:336
  676.6 19.0 %collective-permute-start.9 = (bf16[1,64,16,128]{3,2,1,0:T(8,128)(2,1)S(1)}, bf16[1,64,16,128]{3,2,1,0:T(8,128)(2,1)S(1)}, u32[]{:S(2)}, u32[]{:S(2)}) collective-permute-start(bf16[1,64,16,128]{3,2,1,0:T(8,128)(2,1)S(1)} %dynamic-slice_bitcast_fusion.20), channel_id=1, source_target_pairs={{3,11},{7,15},{11,3},{15,7},{19,27},{23,31},{27,19},{31,23}} | collective-permute-start | bytes 786440 | tf_op jit(solution)/shard_map/ppermute | solution.py:336
  679.5 27.4 %collective-permute-start.11 = (bf16[1,64,16,128]{3,2,1,0:T(8,128)(2,1)S(1)}, bf16[1,64,16,128]{3,2,1,0:T(8,128)(2,1)S(1)}, u32[]{:S(2)}, u32[]{:S(2)}) collective-permute-start(bf16[1,64,16,128]{3,2,1,0:T(8,128)(2,1)S(1)} %dynamic-slice_bitcast_fusion.18), channel_id=1, source_target_pairs={{3,15},{7,11},{11,7},{15,3},{19,31},{23,27},{27,23},{31,19}} | collective-permute-start | bytes 786440 | tf_op jit(solution)/shard_map/ppermute | solution.py:336
  686.9 22.2 %collective-permute-start.12 = (bf16[1,64,16,128]{3,2,1,0:T(8,128)(2,1)S(1)}, bf16[1,64,16,128]{3,2,1,0:T(8,128)(2,1)S(1)}, u32[]{:S(2)}, u32[]{:S(2)}) collective-permute-start(bf16[1,64,16,128]{3,2,1,0:T(8,128)(2,1)S(1)} %get-tuple-element.42), channel_id=1, source_target_pairs={{3,27},{7,31},{11,19},{15,23},{19,11},{23,15},{27,3},{31,7}} | collective-permute-start | bytes 786440 | tf_op jit(solution)/shard_map/ppermute | solution.py:336
  690.8 19.1 %collective-permute-start.13 = (bf16[1,64,16,128]{3,2,1,0:T(8,128)(2,1)S(1)}, bf16[1,64,16,128]{3,2,1,0:T(8,128)(2,1)S(1)}, u32[]{:S(2)}, u32[]{:S(2)}) collective-permute-start(bf16[1,64,16,128]{3,2,1,0:T(8,128)(2,1)S(1)} %get-tuple-element.41), channel_id=1, source_target_pairs={{3,31},{7,27},{11,23},{15,19},{19,15},{23,11},{27,7},{31,3}} | collective-permute-start | bytes 786440 | tf_op jit(solution)/shard_map/ppermute | solution.py:336
  710.6 48.6 %all-to-all-start.2 = ((bf16[8,1,64,16,128]{4,3,2,1,0:T(8,128)(2,1)}), bf16[8,1,64,16,128]{4,3,2,1,0:T(8,128)(2,1)S(1)}, u32[]{:S(2)}, u32[]{:S(2)}) async-start(bf16[8,1,64,16,128]{4,3,2,1,0:T(8,128)(2,1)} %slice.75), calls=%async_computation.2 | async-start | bytes 4194304 | tf_op jit(solution)/shard_map/all_to_all | solution.py:351
  759.2 1.4 copy-start.1
Sparse Core Ops, SparseCore 0:
  8.9 202.2 all-gather.2
  212.8 201.5 all-gather.4
